TPU v7x, 32 devices: a whole 2x2x4 slice. The times are simulated.
32 devices in a mesh: group: 16 (over z, y, core), dp: 2 (over x).
Axes of the slice: x: 2, y: 2, z: 4, core: 2. Of those that a mesh axis runs over, the one named last changes fastest.
Arguments:
- tokens: bfloat16 [4096, 3584], P(('group', 'dp')), may hold values from -6 to 6
- routes: int32 [4096, 1], P(('group', 'dp')), may hold values from 0 to 7; in each aligned block of 128 rows (0 to 127, 128 to 255, ...) at most 24 rows name the same one
- gate_scale: float32 [4096, 1], P(('group', 'dp')), may hold values from 0.1 to 1
- cotangent: bfloat16 [4096, 3584], P(('group', 'dp')), may hold values from -0.59765625 to 0.59765625
- master: float32 [16, 512, 10752], P('group', 'dp'), may hold values from -0.09375 to 0.09375
- moment_one: float32 [16, 512, 10752], P('group', 'dp'), may hold values from -3 to 3
- moment_two: float32 [16, 512, 10752], P('group', 'dp'), may hold values from 0.01 to 1
- dec_tokens: bfloat16 [4, 256, 3584], P(None, 'group'), may hold values from -6 to 6
- dec_routes: int32 [4, 256, 1], P(None, 'group'), may hold values from 0 to 7; in each aligned block of 16 rows (0 to 15, 16 to 31, ..., all dimensions but the last counted through in order) at most 4 rows name the same one
- dec_scale: float32 [4, 256, 1], P(None, 'group'), may hold values from 0.5 to 2
Outputs:
- new_master: float32 [16, 512, 10752], P('group', 'dp')
- new_moment_one: float32 [16, 512, 10752], P('group', 'dp')
- new_moment_two: float32 [16, 512, 10752], P('group', 'dp')
- dec_out: bfloat16 [4, 256, 3584], P(None, 'group', 'dp')
Inputs may be any that keep to these rules, and one draw needn't show every extreme that they name: `routes`: in each aligned block of 128 rows (the rows of one device) no expert is named by more than 24 rows; in some blocks one expert is named by exactly 24. `dec_routes`: within one step, in each aligned block of 16 rows (the rows of one index of group) no expert is named by more than 4 rows; in some blocks one expert is named by exactly 4.
All inputs are finite; a program needn't handle non-finite values.
Results may differ from a plain program's by a relative error of at most 0.0076.
Values may be sent and summed in bfloat16 or wider, within the bound.
A program may use at most 192 MiB of HBM per device.

v0:
```python
import jax
import jax.numpy as jnp
from jax import lax
from jax.sharding import PartitionSpec as P

EXPERTS = 8
CAP = 24
DCAP = 4


adam_lr = 0.001
beta_one = 0.9
beta_two = 0.95
adam_eps = 1e-08
decay_rate = 0.1
step_count = 100.0


def shifted(value, axis, by):
    count = lax.axis_size(axis)
    return lax.ppermute(value, axis, [(i, (i + by) % count) for i in range(count)])


def silu_parts(values):
    sig = jax.nn.sigmoid(values)
    return (values * sig, sig * (1.0 + values * (1.0 - sig)))


def rank_within(route_ids, experts, axis_dim):
    onehot = (route_ids[..., None] == jnp.arange(experts, dtype=jnp.int32)).astype(jnp.int32)
    running = jnp.cumsum(onehot, axis=axis_dim) - 1
    return jnp.sum(running * onehot, axis=-1)


def send_rows(value):
    return lax.all_to_all(value, "group", split_axis=1, concat_axis=1, tiled=True)


def from_peers(value, experts, split, axis_dim):
    parts = [value]
    for offset in range(1, split):
        parts.append(shifted(value, "group", offset * experts))
    return jnp.concatenate(parts, axis_dim)


def contract_rows(left, right):
    return lax.dot_general(
        left, right, (((1,), (1,)), ((), ())), preferred_element_type=jnp.float32
    )


def shards(
    tokens,
    routes,
    gate_scale,
    cotangent,
    master,
    moment_one,
    moment_two,
    dec_tokens,
    dec_routes,
    dec_scale,
):
    groups = lax.axis_size("group")
    replicas = lax.axis_size("dp")
    experts = EXPERTS
    split = groups // experts
    width = tokens.shape[1]
    capacity = CAP
    route_ids = routes[:, 0]
    slot_index = rank_within(route_ids, experts, 0)
    scaled = (gate_scale * cotangent.astype(jnp.float32)).astype(jnp.bfloat16)
    position = route_ids * capacity + slot_index
    select = (jnp.arange(experts * capacity, dtype=jnp.int32)[:, None] == position[None, :]).astype(
        jnp.bfloat16
    )
    packed = jnp.stack(
        [
            jnp.dot(select, tokens, preferred_element_type=jnp.float32),
            jnp.dot(select, scaled, preferred_element_type=jnp.float32),
        ],
        0,
    ).astype(jnp.bfloat16)
    packed = packed.reshape(2, 1, experts * capacity, width)
    tiled = jnp.broadcast_to(packed, (2, split, experts * capacity, width)).reshape(
        2, groups, capacity, width
    )
    arrived = send_rows(tiled)
    row_data = arrived.reshape(2, groups * capacity, width)
    x_rows = row_data[0]
    d_rows = row_data[1]
    master_rows = master[0]
    slice_w = lax.all_gather(master_rows.astype(jnp.bfloat16), "dp", axis=0, tiled=True)
    gate_pre = contract_rows(x_rows, slice_w[:, :width])
    up_pre = contract_rows(x_rows, slice_w[:, width : 2 * width])
    back_pre = contract_rows(d_rows, slice_w[:, 2 * width :])
    silu_val, silu_grad = silu_parts(gate_pre)
    activated = (silu_val * up_pre).astype(jnp.bfloat16)
    grad_up = (back_pre * silu_val).astype(jnp.bfloat16)
    grad_gate = (back_pre * up_pre * silu_grad).astype(jnp.bfloat16)
    pieces = []
    for source, operand in ((grad_gate, x_rows), (grad_up, x_rows), (activated, d_rows)):
        pieces.append(
            lax.dot_general(
                source, operand, (((0,), (0,)), ((), ())), preferred_element_type=jnp.float32
            )
        )
    grads = lax.psum_scatter(jnp.concatenate(pieces, 1), "dp", scatter_dimension=0, tiled=True)
    moment_new = beta_one * moment_one[0] + (1.0 - beta_one) * grads
    second_new = beta_two * moment_two[0] + (1.0 - beta_two) * grads * grads
    correct_one = 1.0 - beta_one**step_count
    correct_two = 1.0 - beta_two**step_count
    update = moment_new / correct_one / (jnp.sqrt(second_new / correct_two) + adam_eps)
    master_new = master_rows - adam_lr * (update + decay_rate * master_rows)
    rollout = from_peers(master_new.astype(jnp.bfloat16), experts, split, 0)
    per_peer = DCAP // split
    out_width = width // replicas
    own_index = lax.axis_index("group")
    outputs = []
    for step_index in range(dec_tokens.shape[0]):
        inputs = dec_tokens[step_index : step_index + 1]
        steps_here = inputs.shape[0]
        ids_now = dec_routes[step_index : step_index + 1][..., 0]
        slot_now = rank_within(ids_now, experts, 1)
        block_now = (slot_now // per_peer + own_index) % split
        decode_position = (
            block_now * (experts * per_peer) + ids_now * per_peer + slot_now % per_peer
        )
        decode_select = (
            jnp.arange(groups * per_peer, dtype=jnp.int32)[None, :, None]
            == decode_position[:, None, :]
        ).astype(jnp.bfloat16)
        decode_packed = jnp.einsum(
            "spr,srd->spd", decode_select, inputs, preferred_element_type=jnp.float32
        ).astype(jnp.bfloat16)
        decode_arrived = send_rows(decode_packed.reshape(steps_here, groups, per_peer, width))
        dec_rows = decode_arrived.reshape(steps_here * groups * per_peer, width)
        dec_gate = contract_rows(dec_rows, rollout[:, :width])
        dec_up = contract_rows(dec_rows, rollout[:, width : 2 * width])
        dec_silu, unused_grad = silu_parts(dec_gate)
        dec_act = (dec_silu * dec_up).astype(jnp.bfloat16)
        down_columns = lax.dynamic_slice_in_dim(
            rollout, 2 * width, out_width * lax.axis_size("dp"), 1
        )
        summed = lax.psum_scatter(
            lax.dot_general(
                down_columns, dec_act, (((0,), (1,)), ((), ())), preferred_element_type=jnp.float32
            ),
            "dp",
            scatter_dimension=0,
            tiled=True,
        )
        expert_out = summed.T.astype(jnp.bfloat16).reshape(steps_here, groups, per_peer, out_width)
        returned = send_rows(expert_out).reshape(steps_here, groups * per_peer, out_width)
        picked = jnp.einsum(
            "spr,spd->srd", decode_select, returned, preferred_element_type=jnp.float32
        )
        outputs.append((dec_scale[step_index : step_index + 1] * picked).astype(jnp.bfloat16))
    dec_out = jnp.concatenate(outputs, 0)
    return (master_new[None], moment_new[None], second_new[None], dec_out)


def solution(mesh):
    in_specs = (
        P(("group", "dp"), None),
        P(("group", "dp"), None),
        P(("group", "dp"), None),
        P(("group", "dp"), None),
        P("group", "dp", None),
        P("group", "dp", None),
        P("group", "dp", None),
        P(None, "group", None),
        P(None, "group", None),
        P(None, "group", None),
    )
    out_specs = (
        P("group", "dp", None),
        P("group", "dp", None),
        P("group", "dp", None),
        P(None, "group", "dp"),
    )
    return jax.shard_map(shards, mesh=mesh, in_specs=in_specs, out_specs=out_specs, check_vma=False)
```

profile of v0, /device:TPU:0, one launch (start us, length us, event | category | flops | bytes accessed | tf_op | source)
XLA Modules:
  0.0 833.1 jit_solution(9864386208292161978)
XLA Ops:
  15.7 7.4 all-to-all-start
  23.2 7.1 bitcast_convert_fusion
  30.5 93.1 %all-to-all-done = bf16[2,16,24,3584]{3,2,0,1:T(8,128)(2,1)} async-done(((bf16[2,16,24,3584]{3,2,0,1:T(8,128)(2,1)}), bf16[2,16,24,3584]{3,2,0,1:T(8,128)(2,1)}, u32[]{:S(2)}, u32[]{:S(2)}) %all-to-all-start) | async-done | bytes 5505056 | tf_op jit(solution)/shard_map/all_to_all | solution.py:36
  123.6 5.4 fusion.98
  129.1 37.9 %all-gather.2.cloned.1.call-done = bf16[512,10752]{1,0:T(8,128)(2,1)} async-done(((bf16[256,10752]{1,0:T(8,128)(2,1)}), bf16[512,10752]{1,0:T(8,128)(2,1)}) %all-gather.2.cloned.1.call-update) | async-done | bytes 11010064 | tf_op jit(solution)/shard_map/all_gather | solution.py:93
  167.0 4.6 fusion.9
  171.7 3.8 fusion.7
  177.7 3.6 fusion.11
  185.8 7.9 pad_maximum_fusion
  193.8 245.6 %reduce-scatter.6.cloned.1.call-done = f32[256,10752]{1,0:T(8,128)} async-done(((f32[512,10752]{1,0:T(8,128)}), f32[256,10752]{1,0:T(8,128)}) %reduce-scatter.6.cloned.1.call-update) | async-done | bytes 11010064 | tf_op jit(solution)/shard_map/reduce_scatter | solution.py:108
  439.4 28.8 %fusion.97 = (bf16[256,10752]{1,0:T(8,128)(2,1)}, f32[256,10752]{1,0:T(8,128)}, f32[1,256,10752]{2,1,0:T(8,128)}, f32[1,256,10752]{2,1,0:T(8,128)}) fusion(f32[256,10752]{1,0:T(8,128)} %reduce-scatter.6.cloned.1.call-done, f32[1,256,10752]{2,1,0:T(8,128)} %param.16, f32[1,256,10752]{2,1,0:T(8,128)} %param.15, f32[1,256,10752]{2,1,0:T(8,128)} %param.14), kind=kLoop, calls=%fused_computation.179 | loop fusion | flops 44040192 | bytes 82575360 | tf_op jit(solution)/shard_map/convert_element_type | solution.py:115
  472.6 3.8 all-to-all-start.7
  477.5 234.9 %all-to-all-done.7 = bf16[1,16,2,3584]{3,2,0,1:T(2,128)(2,1)S(1)} async-done(((bf16[1,16,2,3584]{3,2,0,1:T(2,128)(2,1)}), bf16[1,16,2,3584]{3,2,0,1:T(2,128)(2,1)S(1)}, u32[]{:S(2)}, u32[]{:S(2)}) %all-to-all-start.7) | async-done | bytes 229408 | tf_op jit(solution)/shard_map/all_to_all | solution.py:36
  712.4 5.7 all-to-all-start.5
  718.2 7.1 fusion.6
  728.2 5.8 fusion.45
  735.2 6.0 all-to-all-start.3
  741.4 3.2 fusion.109
  744.6 5.8 fusion.44
  751.5 6.0 all-to-all-start.1
  757.7 3.2 fusion.108
  760.9 5.9 fusion.43
  767.3 3.2 fusion.107
  770.4 6.0 fusion.42
  778.2 6.0 all-to-all-start.8
  785.9 6.0 all-to-all-done.8
  791.9 3.5 all-to-all-start.6
  797.1 6.0 all-to-all-done.6
  803.0 3.5 all-to-all-start.4
  808.5 5.7 all-to-all-done.4
  814.2 3.5 all-to-all-start.2
  818.1 7.2 all-to-all-done.2
  (92 shorter events, 35.3 us)
Async XLA Ops:
  7.2 2.5 copy-start
  15.7 107.9 %all-to-all-start = ((bf16[2,16,24,3584]{3,2,0,1:T(8,128)(2,1)}), bf16[2,16,24,3584]{3,2,0,1:T(8,128)(2,1)}, u32[]{:S(2)}, u32[]{:S(2)}) async-start(bf16[2,16,24,3584]{3,2,0,1:T(8,128)(2,1)} %copy.22), calls=%async_computation | async-start | bytes 11010048 | tf_op jit(solution)/shard_map/all_to_all | solution.py:36
  23.1 143.9 %all-gather.2.cloned.1.call-start = ((), (), s32[]{:S(2)}) async-start(), calls=%async_computation.14 | async-start | bytes 16515072 | tf_op jit(solution)/shard_map/all_gather | solution.py:93
  30.3 409.1 %reduce-scatter.6.cloned.1.call-start = ((), (), s32[]{:S(2)}) async-start(), calls=%async_computation.15 | async-start | bytes 33030144 | tf_op jit(solution)/shard_map/reduce_scatter | solution.py:108
  167.0 4.6 copy-start.3
  171.6 3.8 copy-start.4
  193.7 276.9 %copy-start.6 = (s32[4,16,1]{1,2,0:T(1,128)S(1)}, s32[4,16,1]{1,2,0:T(1,128)}, u32[]{:S(2)}) copy-start(s32[4,16,1]{1,2,0:T(1,128)} %param.18) | copy-start | bytes 772
  193.8 277.7 %copy-start.5 = (bf16[4,16,3584]{2,1,0:T(8,128)(2,1)S(1)}, bf16[4,16,3584]{2,1,0:T(8,128)(2,1)}, u32[]{:S(2)}) copy-start(bf16[4,16,3584]{2,1,0:T(8,128)(2,1)} %param.17) | copy-start | bytes 1376260
  468.2 250.0 %collective-permute-start = (bf16[256,10752]{1,0:T(8,128)(2,1)}, bf16[256,10752]{1,0:T(8,128)(2,1)}, u32[]{:S(2)}, u32[]{:S(2)}) collective-permute-start(bf16[256,10752]{1,0:T(8,128)(2,1)} %get-tuple-element.4), channel_id=1, source_target_pairs={{0,16},{2,18},{4,20},{6,22},{8,24},{10,26},{12,28},{14,30},{16,0},... | collective-permute-start | bytes 16515080 | tf_op jit(solution)/shard_map/ppermute | solution.py:21
  472.6 239.8 %all-to-all-start.7 = ((bf16[1,16,2,3584]{3,2,0,1:T(2,128)(2,1)}), bf16[1,16,2,3584]{3,2,0,1:T(2,128)(2,1)S(1)}, u32[]{:S(2)}, u32[]{:S(2)}) async-start(bf16[1,16,2,3584]{3,2,0,1:T(2,128)(2,1)} %bitcast.41), calls=%async_computation.11 | async-start | bytes 458752 | tf_op jit(solution)/shard_map/all_to_all | solution.py:36
  712.4 22.8 %all-to-all-start.5 = ((bf16[1,16,2,3584]{3,2,0,1:T(2,128)(2,1)}), bf16[1,16,2,3584]{3,2,0,1:T(2,128)(2,1)S(1)}, u32[]{:S(2)}, u32[]{:S(2)}) async-start(bf16[1,16,2,3584]{3,2,0,1:T(2,128)(2,1)} %bitcast.33), calls=%async_computation.8 | async-start | bytes 458752 | tf_op jit(solution)/shard_map/all_to_all | solution.py:36
  718.1 58.4 %reduce-scatter.14.cloned.1.call-start = ((), (), s32[]{:S(2)}) async-start(), calls=%async_computation.19 | async-start | bytes 688128 | tf_op jit(solution)/shard_map/reduce_scatter | solution.py:145
  725.3 1.8 copy-start.2
  735.2 16.3 %all-to-all-start.3 = ((bf16[1,16,2,3584]{3,2,0,1:T(2,128)(2,1)}), bf16[1,16,2,3584]{3,2,0,1:T(2,128)(2,1)S(1)}, u32[]{:S(2)}, u32[]{:S(2)}) async-start(bf16[1,16,2,3584]{3,2,0,1:T(2,128)(2,1)} %bitcast.25), calls=%async_computation.5 | async-start | bytes 458752 | tf_op jit(solution)/shard_map/all_to_all | solution.py:36
  741.2 43.0 %reduce-scatter.12.cloned.1.call-start = ((), (), s32[]{:S(2)}) async-start(), calls=%async_computation.18 | async-start | bytes 688128 | tf_op jit(solution)/shard_map/reduce_scatter | solution.py:145
  751.5 15.6 %all-to-all-start.1 = ((bf16[1,16,2,3584]{3,2,0,1:T(2,128)(2,1)}), bf16[1,16,2,3584]{3,2,0,1:T(2,128)(2,1)S(1)}, u32[]{:S(2)}, u32[]{:S(2)}) async-start(bf16[1,16,2,3584]{3,2,0,1:T(2,128)(2,1)} %bitcast.17), calls=%async_computation.2 | async-start | bytes 458752 | tf_op jit(solution)/shard_map/all_to_all | solution.py:36
  757.6 37.8 %reduce-scatter.10.cloned.1.call-start = ((), (), s32[]{:S(2)}) async-start(), calls=%async_computation.17 | async-start | bytes 688128 | tf_op jit(solution)/shard_map/reduce_scatter | solution.py:145
  760.9 6.2 copy-start.7
  766.8 39.7 %reduce-scatter.8.cloned.1.call-start = ((), (), s32[]{:S(2)}) async-start(), calls=%async_computation.16 | async-start | bytes 688128 | tf_op jit(solution)/shard_map/reduce_scatter | solution.py:145
  770.4 55.9 %copy-start.1 = (bf16[128,3584]{1,0:T(8,128)(2,1)S(1)}, bf16[128,3584]{1,0:T(8,128)(2,1)}, u32[]{:S(2)}) copy-start(bf16[128,3584]{1,0:T(8,128)(2,1)} %param.10) | copy-start | bytes 2752516
  778.2 13.7 %all-to-all-start.8 = ((bf16[1,16,2,1792]{3,2,0,1:T(2,128)(2,1)}), bf16[1,16,2,1792]{3,2,0,1:T(2,128)(2,1)S(1)}, u32[]{:S(2)}, u32[]{:S(2)}) async-start(bf16[1,16,2,1792]{3,2,0,1:T(2,128)(2,1)} %bitcast.43), calls=%async_computation.13 | async-start | bytes 229376 | tf_op jit(solution)/shard_map/all_to_all | solution.py:36
  791.9 11.2 %all-to-all-start.6 = ((bf16[1,16,2,1792]{3,2,0,1:T(2,128)(2,1)}), bf16[1,16,2,1792]{3,2,0,1:T(2,128)(2,1)S(1)}, u32[]{:S(2)}, u32[]{:S(2)}) async-start(bf16[1,16,2,1792]{3,2,0,1:T(2,128)(2,1)} %bitcast.35), calls=%async_computation.10 | async-start | bytes 229376 | tf_op jit(solution)/shard_map/all_to_all | solution.py:36
  803.0 11.2 %all-to-all-start.4 = ((bf16[1,16,2,1792]{3,2,0,1:T(2,128)(2,1)}), bf16[1,16,2,1792]{3,2,0,1:T(2,128)(2,1)S(1)}, u32[]{:S(2)}, u32[]{:S(2)}) async-start(bf16[1,16,2,1792]{3,2,0,1:T(2,128)(2,1)} %bitcast.27), calls=%async_computation.7 | async-start | bytes 229376 | tf_op jit(solution)/shard_map/all_to_all | solution.py:36
  814.2 11.2 %all-to-all-start.2 = ((bf16[1,16,2,1792]{3,2,0,1:T(2,128)(2,1)}), bf16[1,16,2,1792]{3,2,0,1:T(2,128)(2,1)S(1)}, u32[]{:S(2)}, u32[]{:S(2)}) async-start(bf16[1,16,2,1792]{3,2,0,1:T(2,128)(2,1)} %bitcast.19), calls=%async_computation.4 | async-start | bytes 229376 | tf_op jit(solution)/shard_map/all_to_all | solution.py:36
Sparse Core Ops, SparseCore 0:
  30.4 136.5 all-gather.1
  193.9 245.4 reduce-scatter.5
  734.2 14.2 reduce-scatter.13
  750.7 14.0 reduce-scatter.11
  766.9 14.2 reduce-scatter.9
  783.4 13.8 reduce-scatter.7
where the time goes:
time: 834 us; the launch traced here: 833 us
  waiting for transfers between devices  637 us (76%)
  other arithmetic  59 us (7%)
  matrix products  57.4 us (7%)
  starting transfers between devices  48.5 us (6%)
  local copies, waits for them, and re-layouts  17.2 us (2%)
  between operations  14.5 us (2%)
    all_to_all x9, waiting for transfers between devices, send_rows(): lax.all_to_all(value, 'group', split_axis=1, concat_axis=1, tiled=True)  353 us
    reduce_scatter x1, waiting for transfers between devices, shards(): lax.psum_scatter(jnp.concatenate(pieces, 1), 'dp', scatter_dimension=0, t...  246 us
    all_to_all x9, starting transfers between devices, send_rows(): lax.all_to_all(value, 'group', split_axis=1, concat_axis=1, tiled=True)  45.4 us
    all_gather x1, waiting for transfers between devices, shards(): lax.all_gather(master_rows.astype(jnp.bfloat16), 'dp', axis=0, tiled=True)  37.9 us
    convert_element_type x1, other arithmetic, shards(): rollout = from_peers(master_new.astype(jnp.bfloat16), experts, split, 0)  28.8 us
    dot_general x4, matrix products, shards(): lax.dot_general(down_columns, dec_act, (((0,), (1,)), ((), ())), preferre...  23.6 us
    dot_general x7, matrix products, contract_rows(): lax.dot_general(left, right, (((1,), (1,)), ((), ())), preferred_element_...  22.8 us
  transfers between devices with their start and end apart: 16, of which 8 were waited for; matrix products, arithmetic and copies ran while one was open for 8% of the time, Pallas kernels for 0%

commit v1 on v0

--- a/solution.py
+++ b/solution.py
@@ -1,6 +1,10 @@
+import functools
+
 import jax
 import jax.numpy as jnp
 from jax import lax
+from jax.experimental import pallas as pl
+from jax.experimental.pallas import tpu as pltpu
 from jax.sharding import PartitionSpec as P
 
 EXPERTS = 8
@@ -160,6 +164,536 @@
     return (master_new[None], moment_new[None], second_new[None], dec_out)
 
 
+MESH = pl.DeviceIdType.MESH
+CONTRACT_MINOR = (((1,), (1,)), ((), ()))
+CONTRACT_MAJOR = (((0,), (0,)), ((), ()))
+
+
+def pick_tile(width):
+    return 512 if width % 512 == 0 else 128
+
+
+def greet_peers(own_group, own_dp, groups):
+    barrier = pltpu.get_barrier_semaphore()
+    for step in range(1, groups):
+        pl.semaphore_signal(
+            barrier,
+            inc=1,
+            device_id={"group": lax.rem(own_group + step, groups), "dp": own_dp},
+            device_id_type=MESH,
+        )
+    pl.semaphore_signal(
+        barrier, inc=1, device_id={"group": own_group, "dp": 1 - own_dp}, device_id_type=MESH
+    )
+    pl.semaphore_wait(barrier, groups)
+
+
+def learner_kernel(
+    groups,
+    tok,
+    cot,
+    gate_scale,
+    sel,
+    dtok,
+    dsel,
+    master,
+    grads,
+    drows_out,
+    packed,
+    rows,
+    dpacked,
+    drows,
+    weights,
+    pre,
+    left,
+    near_send,
+    near_recv,
+    half_send,
+    half_recv,
+    side_send,
+    side_recv,
+    dnear_send,
+    dnear_recv,
+    dhalf_send,
+    dhalf_recv,
+    dside_send,
+    dside_recv,
+    out_sem,
+):
+    group = lax.axis_index("group")
+    dp = lax.axis_index("dp")
+    half = group // EXPERTS
+    expert = lax.rem(group, EXPERTS)
+    width = tok.shape[1]
+    hidden = weights.shape[0]
+    tile = pick_tile(width)
+    block = 2 * CAP
+    chunk = EXPERTS * block
+
+    def remote(src, dst, send, recv, to_group, to_dp):
+        return pltpu.make_async_remote_copy(
+            src_ref=src,
+            dst_ref=dst,
+            send_sem=send,
+            recv_sem=recv,
+            device_id={"group": to_group, "dp": to_dp},
+            device_id_type=MESH,
+        )
+
+    @pl.loop(0, width // tile)
+    def _(index):
+        columns = pl.ds(pl.multiple_of(index * tile, tile), tile)
+        scaled = (gate_scale[...] * cot[:, columns].astype(jnp.float32)).astype(jnp.bfloat16)
+        both = jnp.concatenate([tok[:, columns], scaled], 0)
+        picked = jnp.dot(sel[...], both, preferred_element_type=jnp.float32).astype(jnp.bfloat16)
+        packed[:, :, columns] = picked.reshape(EXPERTS, block, tile)
+        picked = jnp.dot(dsel[...], dtok[:, columns], preferred_element_type=jnp.float32)
+        dpacked[:, :, columns] = picked.astype(jnp.bfloat16).reshape(EXPERTS, -1, tile)
+
+    greet_peers(group, dp, groups)
+
+    near = [None] + [
+        remote(
+            packed.at[lax.rem(expert + step, EXPERTS)],
+            rows.at[0, 0, step],
+            near_send.at[step],
+            near_recv.at[step],
+            half * EXPERTS + lax.rem(expert + step, EXPERTS),
+            dp,
+        )
+        for step in range(1, EXPERTS)
+    ]
+    other_group = (1 - half) * EXPERTS + expert
+    across = []
+    beside = []
+    for step in range(EXPERTS):
+        source = packed.at[expert] if step == 0 else rows.at[0, 0, step]
+        across.append(
+            remote(
+                source,
+                rows.at[0, 1, step],
+                half_send.at[step],
+                half_recv.at[step],
+                other_group,
+                dp,
+            )
+        )
+        beside.append(
+            remote(
+                source,
+                rows.at[1, 0, step],
+                side_send.at[0, step],
+                side_recv.at[0, step],
+                group,
+                1 - dp,
+            )
+        )
+    further = [
+        remote(
+            rows.at[0, 1, step],
+            rows.at[1, 1, step],
+            side_send.at[1, step],
+            side_recv.at[1, step],
+            group,
+            1 - dp,
+        )
+        for step in range(EXPERTS)
+    ]
+    dnear = [None] + [
+        remote(
+            dpacked.at[lax.rem(expert + step, EXPERTS)],
+            drows.at[0, step],
+            dnear_send.at[step],
+            dnear_recv.at[step],
+            half * EXPERTS + lax.rem(expert + step, EXPERTS),
+            dp,
+        )
+        for step in range(1, EXPERTS)
+    ]
+    dacross = []
+    dbeside = []
+    for index in range(EXPERTS // 2):
+        step = 2 * index + dp
+        dacross.append(
+            remote(
+                dpacked.at[lax.rem(expert + step, EXPERTS)],
+                drows.at[1, step],
+                dhalf_send.at[index],
+                dhalf_recv.at[index],
+                (1 - half) * EXPERTS + lax.rem(expert + step, EXPERTS),
+                dp,
+            )
+        )
+        dbeside.append(
+            remote(
+                drows.at[1, step],
+                drows.at[1, step],
+                dside_send.at[index],
+                dside_recv.at[index],
+                group,
+                1 - dp,
+            )
+        )
+
+    across[0].start()
+    beside[0].start()
+    for step in range(1, EXPERTS):
+        near[step].start()
+    rows[0, 0, 0] = packed[expert]
+    drows[0, 0] = dpacked[expert]
+
+    lines = min(16, hidden)
+
+    def cast_body(source):
+        begin = pl.multiple_of(pl.program_id(0) * lines, lines)
+        weights[pl.ds(begin, lines), :] = source[...].astype(jnp.bfloat16)
+
+    pltpu.emit_pipeline(
+        cast_body,
+        grid=(hidden // lines,),
+        in_specs=[pl.BlockSpec((lines, 3 * width), lambda i: (i, 0))],
+        out_specs=[],
+    )(master)
+
+    for step in range(1, EXPERTS):
+        near[step].wait_recv()
+        across[step].start()
+        beside[step].start()
+
+    def learn(side, far, first):
+        own = rows.at[side, far]
+        pre[...] = jnp.zeros_like(pre)
+
+        @pl.loop(0, width // tile)
+        def _(index):
+            start = pl.multiple_of(index * tile, tile)
+            operand = own[:, :, pl.ds(start, tile)].reshape(chunk, tile)
+            for part in range(3):
+                begin = pl.multiple_of(part * width + start, 128)
+                pre[:, part * hidden : (part + 1) * hidden] += lax.dot_general(
+                    operand,
+                    weights[:, pl.ds(begin, tile)],
+                    CONTRACT_MINOR,
+                    preferred_element_type=jnp.float32,
+                )
+
+        parts = pre[...].reshape(EXPERTS, block, 3 * hidden)
+        gate_pre = parts[:, :CAP, :hidden]
+        up_pre = parts[:, :CAP, hidden : 2 * hidden]
+        back_pre = parts[:, CAP:, 2 * hidden :]
+        silu_val, silu_grad = silu_parts(gate_pre)
+        zeros = jnp.zeros_like(gate_pre)
+        top = jnp.concatenate([back_pre * up_pre * silu_grad, back_pre * silu_val, zeros], 2)
+        bottom = jnp.concatenate([zeros, zeros, silu_val * up_pre], 2)
+        left[...] = (
+            jnp.concatenate([top, bottom], 1)
+            .reshape(chunk, 3 * hidden)
+            .T.astype(jnp.bfloat16)
+        )
+
+        @pl.loop(0, width // tile)
+        def _(index):
+            columns = pl.ds(pl.multiple_of(index * tile, tile), tile)
+            operand = own[:, :, columns].reshape(chunk, tile)
+            value = jnp.dot(left[...], operand, preferred_element_type=jnp.float32)
+            if first:
+                grads[:, columns] = value
+            else:
+                grads[:, columns] += value
+
+    learn(0, 0, True)
+    for step in range(EXPERTS):
+        across[step].wait_recv()
+        further[step].start()
+        if step == EXPERTS - 3:
+            for index in range(EXPERTS // 2):
+                dacross[index].start()
+            for other in range(1, EXPERTS):
+                dnear[other].start()
+    for step in range(EXPERTS):
+        beside[step].wait_recv()
+    learn(1, 0, False)
+    for index in range(EXPERTS // 2):
+        dacross[index].wait_recv()
+        dbeside[index].start()
+    learn(0, 1, False)
+    for step in range(EXPERTS):
+        further[step].wait_recv()
+    learn(1, 1, False)
+    for step in range(1, EXPERTS):
+        dnear[step].wait_recv()
+    for index in range(EXPERTS // 2):
+        step = 2 * index + 1 - dp
+        remote(
+            drows.at[1, step],
+            drows.at[1, step],
+            dside_send.at[index],
+            dside_recv.at[index],
+            group,
+            1 - dp,
+        ).wait_recv()
+    leave = pltpu.make_async_copy(drows, drows_out, out_sem)
+    leave.start()
+    leave.wait()
+    for step in range(EXPERTS):
+        across[step].wait_send()
+        beside[step].wait_send()
+        further[step].wait_send()
+        if step:
+            near[step].wait_send()
+            dnear[step].wait_send()
+    for index in range(EXPERTS // 2):
+        dacross[index].wait_send()
+        dbeside[index].wait_send()
+
+
+def decode_kernel(
+    groups,
+    drows,
+    roll,
+    dsel,
+    dscale,
+    out,
+    pre,
+    own,
+    side_out,
+    side_in,
+    back_out,
+    back_in,
+    side_send,
+    side_recv,
+    back_send,
+    back_recv,
+):
+    group = lax.axis_index("group")
+    dp = lax.axis_index("dp")
+    half = group // EXPERTS
+    expert = lax.rem(group, EXPERTS)
+    hidden, wide = roll.shape
+    width = wide // 3
+    out_width = width // 2
+    tile = pick_tile(width)
+    slots = drows.shape[0] // (2 * EXPERTS)
+    pieces = side_out.shape[0]
+    per_piece = 2 * EXPERTS // pieces
+    greet_peers(group, dp, groups)
+    pre[...] = jnp.zeros_like(pre)
+
+    @pl.loop(0, width // tile)
+    def _(index):
+        start = pl.multiple_of(index * tile, tile)
+        operand = drows[:, pl.ds(start, tile)]
+        for part in range(2):
+            begin = pl.multiple_of(part * width + start, 128)
+            pre[:, part * hidden : (part + 1) * hidden] += lax.dot_general(
+                operand,
+                roll[:, pl.ds(begin, tile)],
+                CONTRACT_MINOR,
+                preferred_element_type=jnp.float32,
+            )
+
+    dec_silu, unused_grad = silu_parts(pre[:, :hidden])
+    act = (dec_silu * pre[:, hidden:]).astype(jnp.bfloat16)
+    strip = 256 if out_width % 256 == 0 else 128
+    for index in range(out_width // strip):
+        begin = pl.multiple_of(2 * width + (1 - dp) * out_width + index * strip, 128)
+        value = jnp.dot(act, roll[:, pl.ds(begin, strip)], preferred_element_type=jnp.float32)
+        side_out[:, :, index * strip : (index + 1) * strip] = value.astype(jnp.bfloat16).reshape(
+            pieces, -1, strip
+        )
+    order = list(range(pieces // 2, pieces)) + list(range(pieces // 2))
+    side = [
+        pltpu.make_async_remote_copy(
+            src_ref=side_out.at[piece],
+            dst_ref=side_in.at[piece],
+            send_sem=side_send.at[piece],
+            recv_sem=side_recv.at[piece],
+            device_id={"group": group, "dp": 1 - dp},
+            device_id_type=MESH,
+        )
+        for piece in range(pieces)
+    ]
+    for piece in order:
+        side[piece].start()
+    for index in range(out_width // strip):
+        begin = pl.multiple_of(2 * width + dp * out_width + index * strip, 128)
+        value = jnp.dot(act, roll[:, pl.ds(begin, strip)], preferred_element_type=jnp.float32)
+        own[:, :, index * strip : (index + 1) * strip] = value.reshape(pieces, -1, strip)
+    back = {}
+    for piece in order:
+        side[piece].wait_recv()
+        total = (own[piece] + side_in[piece].astype(jnp.float32)).astype(jnp.bfloat16)
+        total = total.reshape(per_piece, slots, out_width)
+        for place in range(per_piece):
+            far, step = divmod(piece * per_piece + place, EXPERTS)
+            if far == 0 and step == 0:
+                back_in[0, 0] = total[place]
+                continue
+            back_out[far, step] = total[place]
+            to_half = 1 - half if far else half
+            back[far, step] = pltpu.make_async_remote_copy(
+                src_ref=back_out.at[far, step],
+                dst_ref=back_in.at[far, step],
+                send_sem=back_send.at[far, step],
+                recv_sem=back_recv.at[far, step],
+                device_id={
+                    "group": to_half * EXPERTS + lax.rem(expert + EXPERTS - step, EXPERTS),
+                    "dp": dp,
+                },
+                device_id_type=MESH,
+            )
+            back[far, step].start()
+    for copy in back.values():
+        copy.wait_recv()
+    total = (back_in[0].astype(jnp.float32) + back_in[1].astype(jnp.float32)).astype(jnp.bfloat16)
+    total = total.reshape(EXPERTS * slots, out_width)
+    picked = lax.dot_general(
+        dsel[...], total, CONTRACT_MAJOR, preferred_element_type=jnp.float32
+    )
+    out[...] = (dscale[...] * picked).astype(jnp.bfloat16)
+    for copy in back.values():
+        copy.wait_send()
+    for copy in side:
+        copy.wait_send()
+
+
+def moved_rows(
+    tokens,
+    routes,
+    gate_scale,
+    cotangent,
+    master,
+    moment_one,
+    moment_two,
+    dec_tokens,
+    dec_routes,
+    dec_scale,
+):
+    groups = lax.axis_size("group")
+    width = tokens.shape[1]
+    hidden = master.shape[1]
+    steps, dec_here = dec_tokens.shape[:2]
+    slots = steps * DCAP
+    own_expert = lax.rem(lax.axis_index("group"), EXPERTS)
+    route_ids = routes[:, 0]
+    position = route_ids * (2 * CAP) + rank_within(route_ids, EXPERTS, 0)
+    position = jnp.concatenate([position, position + CAP])
+    sel = (
+        jnp.arange(EXPERTS * 2 * CAP, dtype=jnp.int32)[:, None] == position[None, :]
+    ).astype(jnp.bfloat16)
+    dec_ids = dec_routes[..., 0]
+    within = rank_within(dec_ids, EXPERTS, 1) + DCAP * jnp.arange(steps, dtype=jnp.int32)[:, None]
+    dec_place = jnp.arange(EXPERTS * slots, dtype=jnp.int32)[:, None]
+    dsel = (dec_place == (dec_ids * slots + within).reshape(1, -1)).astype(jnp.bfloat16)
+    turned = lax.rem(dec_ids + EXPERTS - own_expert, EXPERTS)
+    back_sel = (dec_place == (turned * slots + within).reshape(1, -1)).astype(jnp.bfloat16)
+
+    master_rows = master[0]
+    vmem = pl.BlockSpec(memory_space=pltpu.VMEM)
+    anywhere = pl.BlockSpec(memory_space=pl.ANY)
+    dma = pltpu.SemaphoreType.DMA
+    rows_all = 2 * 2 * EXPERTS * 2 * CAP
+    grads, drows = pl.pallas_call(
+        functools.partial(learner_kernel, groups),
+        out_shape=(
+            jax.ShapeDtypeStruct((3 * hidden, width), jnp.float32),
+            jax.ShapeDtypeStruct((2, EXPERTS, slots, width), jnp.bfloat16),
+        ),
+        in_specs=[vmem] * 6 + [anywhere],
+        out_specs=(vmem, anywhere),
+        scratch_shapes=[
+            pltpu.VMEM((EXPERTS, 2 * CAP, width), jnp.bfloat16),
+            pltpu.VMEM((2, 2, EXPERTS, 2 * CAP, width), jnp.bfloat16),
+            pltpu.VMEM((EXPERTS, slots, width), jnp.bfloat16),
+            pltpu.VMEM((2, EXPERTS, slots, width), jnp.bfloat16),
+            pltpu.VMEM((hidden, 3 * width), jnp.bfloat16),
+            pltpu.VMEM((EXPERTS * 2 * CAP, 3 * hidden), jnp.float32),
+            pltpu.VMEM((3 * hidden, EXPERTS * 2 * CAP), jnp.bfloat16),
+            dma((EXPERTS,)),
+            dma((EXPERTS,)),
+            dma((EXPERTS,)),
+            dma((EXPERTS,)),
+            dma((2, EXPERTS)),
+            dma((2, EXPERTS)),
+            dma((EXPERTS,)),
+            dma((EXPERTS,)),
+            dma((EXPERTS // 2,)),
+            dma((EXPERTS // 2,)),
+            dma((EXPERTS // 2,)),
+            dma((EXPERTS // 2,)),
+            dma(()),
+        ],
+        compiler_params=pltpu.CompilerParams(
+            collective_id=0, has_side_effects=True, vmem_limit_bytes=56 * 2**20
+        ),
+        cost_estimate=pl.CostEstimate(
+            flops=12 * rows_all * hidden * width,
+            bytes_accessed=24 * hidden * width,
+            transcendentals=rows_all * hidden,
+        ),
+        name="learner",
+    )(
+        tokens,
+        cotangent,
+        gate_scale,
+        sel,
+        dec_tokens.reshape(steps * dec_here, width),
+        dsel,
+        master_rows,
+    )
+    grads = jnp.concatenate(
+        [grads[part * hidden : (part + 1) * hidden] for part in range(3)], 1
+    )
+    moment_new = beta_one * moment_one[0] + (1.0 - beta_one) * grads
+    second_new = beta_two * moment_two[0] + (1.0 - beta_two) * grads * grads
+    correct_one = 1.0 - beta_one**step_count
+    correct_two = 1.0 - beta_two**step_count
+    update = moment_new / correct_one / (jnp.sqrt(second_new / correct_two) + adam_eps)
+    master_new = master_rows - adam_lr * (update + decay_rate * master_rows)
+    rollout = master_new.astype(jnp.bfloat16)
+    out_width = width // 2
+    rows_dec = 2 * EXPERTS * slots
+    pieces = 4
+    dec_out = pl.pallas_call(
+        functools.partial(decode_kernel, groups),
+        out_shape=jax.ShapeDtypeStruct((steps * dec_here, out_width), jnp.bfloat16),
+        in_specs=[vmem] * 4,
+        out_specs=vmem,
+        scratch_shapes=[
+            pltpu.VMEM((rows_dec, 2 * hidden), jnp.float32),
+            pltpu.VMEM((pieces, rows_dec // pieces, out_width), jnp.float32),
+            pltpu.VMEM((pieces, rows_dec // pieces, out_width), jnp.bfloat16),
+            pltpu.VMEM((pieces, rows_dec // pieces, out_width), jnp.bfloat16),
+            pltpu.VMEM((2, EXPERTS, slots, out_width), jnp.bfloat16),
+            pltpu.VMEM((2, EXPERTS, slots, out_width), jnp.bfloat16),
+            dma((pieces,)),
+            dma((pieces,)),
+            dma((2, EXPERTS)),
+            dma((2, EXPERTS)),
+        ],
+        compiler_params=pltpu.CompilerParams(
+            collective_id=1, has_side_effects=True, vmem_limit_bytes=40 * 2**20
+        ),
+        cost_estimate=pl.CostEstimate(
+            flops=6 * rows_dec * hidden * width,
+            bytes_accessed=6 * hidden * width,
+            transcendentals=rows_dec * hidden,
+        ),
+        name="decode",
+    )(
+        drows.reshape(rows_dec, width),
+        rollout,
+        back_sel,
+        dec_scale.reshape(steps * dec_here, 1),
+    )
+    return (
+        master_new[None],
+        moment_new[None],
+        second_new[None],
+        dec_out.reshape(steps, dec_here, out_width),
+    )
+
+
 def solution(mesh):
     in_specs = (
         P(("group", "dp"), None),
@@ -179,4 +713,6 @@
         P("group", "dp", None),
         P(None, "group", "dp"),
     )
-    return jax.shard_map(shards, mesh=mesh, in_specs=in_specs, out_specs=out_specs, check_vma=False)
+    in_place = mesh.shape["group"] == 2 * EXPERTS and mesh.shape["dp"] == 2
+    body = moved_rows if in_place else shards
+    return jax.shard_map(body, mesh=mesh, in_specs=in_specs, out_specs=out_specs, check_vma=False)

time: 834 us -> 277 us (0.33)
  waiting for transfers between devices: 637 us -> 0 us
  Pallas kernels: 0 us -> 208 us
  matrix products: 57.4 us -> 0 us
  starting transfers between devices: 48.5 us -> 0 us
  between operations: 14.5 us -> 0.72 us
  other arithmetic: 59 us -> 48.7 us
    all_to_all x9 -> x0, waiting for transfers between devices: 353 us -> none  [send_rows(): lax.all_to_all(value, 'group', split_axis=1, concat_axis=1, tiled=True)]
    reduce_scatter x5 -> x0, waiting for transfers between devices: 246 us -> none  [the longest x1 246 us: shards(): lax.psum_scatter(jnp.concatenate(pieces, 1), 'dp', scatter_dimension=0, t...]
    pallas_call x0 -> x2, Pallas kernels: none -> 208 us  [the longest x1 172 us: moved_rows(): pl.pallas_call(functools.partial(learner_kernel, groups), out_shape=(jax....]
    dot_general x24 -> x0, matrix products: 57.4 us -> none  [the longest x4 23.6 us: shards(): lax.dot_general(down_columns, dec_act, (((0,), (1,)), ((), ())), preferre...]
    all_to_all x9 -> x0, starting transfers between devices: 45.4 us -> none  [send_rows(): lax.all_to_all(value, 'group', split_axis=1, concat_axis=1, tiled=True)]
    all_gather x1 -> x0, waiting for transfers between devices: 37.9 us -> none  [shards(): lax.all_gather(master_rows.astype(jnp.bfloat16), 'dp', axis=0, tiled=True)]
    sub x0 -> x2, other arithmetic: none -> 28.1 us  [the longest x1 27.4 us: moved_rows(): master_new = master_rows - adam_lr * (update + decay_rate * master_rows)]
    convert_element_type x6 -> x3, other arithmetic: 39.7 us -> 15.1 us  [the longest x1 13.7 us: moved_rows(): rollout = master_new.astype(jnp.bfloat16)]
  transfers between devices with their start and end apart: 16 -> 0, of which waited for: 8 -> 0; matrix products, arithmetic and copies ran while one was open for 8% -> 0% of each run, Pallas kernels for 0% -> 0%
where the time goes in v1:
time: 277 us; the launch traced here: 276 us
  Pallas kernels  208 us (75%)
  other arithmetic  48.7 us (18%)
  local copies, waits for them, and re-layouts  17.7 us (6%)
    pallas_call x1, Pallas kernels, moved_rows(): pl.pallas_call(functools.partial(learner_kernel, groups), out_shape=(jax....  172 us
    pallas_call x1, Pallas kernels, moved_rows(): pl.pallas_call(functools.partial(decode_kernel, groups), out_shape=jax.Sh...  36.9 us
    sub x1, other arithmetic, moved_rows(): master_new = master_rows - adam_lr * (update + decay_rate * master_rows)  27.4 us
    convert_element_type x1, other arithmetic, moved_rows(): rollout = master_new.astype(jnp.bfloat16)  13.7 us
    slice x1, local copies, waits for them, and re-layouts, moved_rows(): grads[part * hidden:(part + 1) * hidden]  13.7 us

profile of v1, /device:TPU:0, one launch (start us, length us, event | category | flops | bytes accessed | tf_op | source)
XLA Modules:
  0.0 275.6 jit_solution(15991436738506976697)
XLA Ops:
  0.6 0.5 broadcast.136
  1.2 1.3 reduce.11
  2.5 0.7 subtract_reduce_fusion
  3.2 0.1 sub.33
  3.3 0.1 mul.126
  3.4 0.1 reshape.208.dscale
  3.5 0.8 fusion.12
  4.3 0.9 select_reduce_fusion.1
  5.2 0.1 broadcast_add_fusion
  5.2 0.1 add.87
  5.3 0.6 fusion.10
  6.0 1.4 copy.14.gate_scale
  7.4 0.7 fusion.9
  8.1 0.2 reduce_window_sum.22
  8.3 0.8 select_reduce_fusion
  9.1 0.7 broadcast_add_fusion.1
  9.8 0.7 fusion.8.sel
  10.5 171.5 %learner.1 = (f32[768,3584]{1,0:T(8,128)}, bf16[2,8,16,3584]{3,2,1,0:T(8,128)(2,1)}) custom-call(bf16[128,3584]{1,0:T(8,128)(2,1)} %tok.1, bf16[128,3584]{1,0:T(8,128)(2,1)} %cot.1, f32[128,1]{1,0:T(8,128)} %copy.14.gate_scale, bf16[384,256]{1,0:T(8,128)(2,1)} %fusion.8.sel, bf16[64,3584]{1,0:T(8,128)(2,1)} %bitcast.35, ...), custom_call_target="tpu_custom_call" | custom-call | flops 16911433728 | bytes 22020096 | tf_op jit(solution)/shard_map/learner/pallas_call | solution.py:596
  182.0 0.0 copy-start.1
  182.1 13.7 %fusion.17 = (f32[256,3584]{1,0:T(8,128)}, f32[1,256,3584]{2,1,0:T(8,128)}, f32[1,256,3584]{2,1,0:T(8,128)}, f32[1,256,3584]{2,1,0:T(8,128)}, f32[256,3584]{1,0:T(8,128)}, /*index=5*/f32[256,3584]{1,0:T(8,128)}) fusion(f32[768,3584]{1,0:T(8,128)} %get-tuple-element.6), kind=kLoop, calls=%fused_computation.43 | loop fusion | bytes 33030144 | tf_op jit(solution)/shard_map/slice | solution.py:645
  195.8 1.1 copy-done.1
  196.9 0.0 copy-start
  196.9 13.7 %subtract_convert_fusion.roll = bf16[256,10752]{1,0:T(8,128)(2,1)S(1)} fusion(f32[256,3584]{1,0:T(8,128)} %get-tuple-element.19, f32[256,3584]{1,0:T(8,128)} %get-tuple-element.20, f32[256,3584]{1,0:T(8,128)} %get-tuple-element.15, f32[1,256,10752]{2,1,0:T(8,128)} %param.16, f32[1,256,10752]{2,1,0:T(8,128)} %param.15, f32[1,256,10752]{2,1,0:T(8,128)S(1)} %copy-done.1), kind=kLoop, calls=%fused_computation.13 | loop fusion | flops 49545216 | bytes 49545216 | tf_op jit(solution)/shard_map/convert_element_type | solution.py:653
  210.6 0.0 copy-done
  210.6 36.9 %decode.1 = bf16[64,1792]{1,0:T(8,128)(2,1)S(1)} custom-call(bf16[256,3584]{1,0:T(8,128)(2,1)S(1)} %bitcast.28, bf16[256,10752]{1,0:T(8,128)(2,1)S(1)} %subtract_convert_fusion.roll, bf16[128,64]{1,0:T(8,128)(2,1)S(1)} %get-tuple-element.24.dsel, f32[64,1]{1,0:T(8,128)S(1)} %reshape.208.dscale), custom_call_target="tpu_custom_call" | custom-call | flops 1409286144 | bytes 5505024 | tf_op jit(solution)/shard_map/decode/pallas_call | solution.py:657
  247.5 27.4 %multiply_subtract_fusion = (f32[1,256,10752]{2,1,0:T(8,128)}, f32[1,256,10752]{2,1,0:T(8,128)}, f32[1,256,10752]{2,1,0:T(8,128)}) fusion(f32[1,256,10752]{2,1,0:T(8,128)} %param.14, f32[1,256,3584]{2,1,0:T(8,128)} %get-tuple-element.18, f32[1,256,3584]{2,1,0:T(8,128)} %get-tuple-element.17, f32[1,256,3584]{2,1,0:T(8,128)} %get-tuple-element.16, ...), kind=kLoop, calls=%fused_computation.14 | loop fusion | flops 46792704 | bytes 77070336 | tf_op jit(solution)/shard_map/sub | solution.py:652
  274.9 0.7 copy.17
  (4 shorter events, 0.1 us)
Async XLA Ops:
  182.0 14.8 %copy-start.1 = (f32[1,256,10752]{2,1,0:T(8,128)S(1)}, f32[1,256,10752]{2,1,0:T(8,128)}, u32[]{:S(2)}) copy-start(f32[1,256,10752]{2,1,0:T(8,128)} %param.14) | copy-start | bytes 33030148
  196.9 13.7 %copy-start = (bf16[2,8,16,3584]{3,2,1,0:T(8,128)(2,1)S(1)}, bf16[2,8,16,3584]{3,2,1,0:T(8,128)(2,1)}, u32[]{:S(2)}) copy-start(bf16[2,8,16,3584]{3,2,1,0:T(8,128)(2,1)} %get-tuple-element.7) | copy-start | bytes 5505028

commit v2 on v1

--- a/solution.py
+++ b/solution.py
@@ -173,6 +173,39 @@
     return 512 if width % 512 == 0 else 128
 
 
+def count_before(ids, group_of):
+    count = ids.shape[1]
+    lines = lax.broadcasted_iota(jnp.int32, (16, count), 0)
+    onehot = (lines == ids).astype(jnp.float32)
+    earlier = lax.broadcasted_iota(jnp.int32, (count, count), 0)
+    later = lax.broadcasted_iota(jnp.int32, (count, count), 1)
+    before = (earlier < later) & (earlier // group_of == later // group_of)
+    running = jnp.dot(
+        onehot.astype(jnp.bfloat16),
+        before.astype(jnp.float32).astype(jnp.bfloat16),
+        preferred_element_type=jnp.float32,
+    )
+    return jnp.sum(running * onehot, axis=0, keepdims=True)
+
+
+def as_column(line):
+    count = line.shape[1]
+    across = lax.broadcasted_iota(jnp.int32, (count, count), 0)
+    along = lax.broadcasted_iota(jnp.int32, (count, count), 1)
+    return jnp.sum(jnp.where(across == along, line, 0.0), axis=1, keepdims=True)
+
+
+def one_hot_rows(count, place):
+    lines = lax.broadcasted_iota(jnp.int32, (count, place.shape[1]), 0).astype(jnp.float32)
+    return (lines == place).astype(jnp.float32).astype(jnp.bfloat16)
+
+
+def decode_place(ids, step_rows, slots, turned):
+    step_of = lax.broadcasted_iota(jnp.int32, ids.shape, 1) // step_rows
+    within = (step_of * DCAP).astype(jnp.float32) + count_before(ids, step_rows)
+    return (turned * slots).astype(jnp.float32) + within
+
+
 def greet_peers(own_group, own_dp, groups):
     barrier = pltpu.get_barrier_semaphore()
     for step in range(1, groups):
@@ -190,15 +223,20 @@
 
 def learner_kernel(
     groups,
+    step_rows,
     tok,
     cot,
+    scale_line,
+    routes,
+    dtok,
+    droutes,
+    master,
+    grads_out,
+    drows_out,
+    grads,
     gate_scale,
     sel,
-    dtok,
     dsel,
-    master,
-    grads,
-    drows_out,
     packed,
     rows,
     dpacked,
@@ -219,6 +257,7 @@
     dside_send,
     dside_recv,
     out_sem,
+    grads_sem,
 ):
     group = lax.axis_index("group")
     dp = lax.axis_index("dp")
@@ -239,6 +278,14 @@
             device_id={"group": to_group, "dp": to_dp},
             device_id_type=MESH,
         )
+
+    gate_scale[...] = as_column(scale_line[...])
+    ids = routes[...]
+    place = (ids * block).astype(jnp.float32) + count_before(ids, ids.shape[1])
+    sel[...] = one_hot_rows(chunk, jnp.concatenate([place, place + CAP], 1))
+    slots = dpacked.shape[1]
+    ids = droutes[...]
+    dsel[...] = one_hot_rows(EXPERTS * slots, decode_place(ids, step_rows, slots, ids))
 
     @pl.loop(0, width // tile)
     def _(index):
@@ -360,24 +407,25 @@
         across[step].start()
         beside[step].start()
 
-    def learn(side, far, first):
-        own = rows.at[side, far]
-        pre[...] = jnp.zeros_like(pre)
+    def learn(side, far, begin_step, steps, first=False, last=False):
+        own = rows.at[side, far, pl.ds(begin_step, steps)]
+        height = steps * block
+        pre[:height] = jnp.zeros((height, 3 * hidden), jnp.float32)
 
         @pl.loop(0, width // tile)
         def _(index):
             start = pl.multiple_of(index * tile, tile)
-            operand = own[:, :, pl.ds(start, tile)].reshape(chunk, tile)
+            operand = own[:, :, pl.ds(start, tile)].reshape(height, tile)
             for part in range(3):
                 begin = pl.multiple_of(part * width + start, 128)
-                pre[:, part * hidden : (part + 1) * hidden] += lax.dot_general(
+                pre[:height, part * hidden : (part + 1) * hidden] += lax.dot_general(
                     operand,
                     weights[:, pl.ds(begin, tile)],
                     CONTRACT_MINOR,
                     preferred_element_type=jnp.float32,
                 )
 
-        parts = pre[...].reshape(EXPERTS, block, 3 * hidden)
+        parts = pre[:height].reshape(steps, block, 3 * hidden)
         gate_pre = parts[:, :CAP, :hidden]
         up_pre = parts[:, :CAP, hidden : 2 * hidden]
         back_pre = parts[:, CAP:, 2 * hidden :]
@@ -385,41 +433,47 @@
         zeros = jnp.zeros_like(gate_pre)
         top = jnp.concatenate([back_pre * up_pre * silu_grad, back_pre * silu_val, zeros], 2)
         bottom = jnp.concatenate([zeros, zeros, silu_val * up_pre], 2)
-        left[...] = (
+        left[:, :height] = (
             jnp.concatenate([top, bottom], 1)
-            .reshape(chunk, 3 * hidden)
+            .reshape(height, 3 * hidden)
             .T.astype(jnp.bfloat16)
         )
 
         @pl.loop(0, width // tile)
         def _(index):
             columns = pl.ds(pl.multiple_of(index * tile, tile), tile)
-            operand = own[:, :, columns].reshape(chunk, tile)
-            value = jnp.dot(left[...], operand, preferred_element_type=jnp.float32)
+            operand = own[:, :, columns].reshape(height, tile)
+            value = jnp.dot(left[:, :height], operand, preferred_element_type=jnp.float32)
             if first:
                 grads[:, columns] = value
             else:
                 grads[:, columns] += value
-
-    learn(0, 0, True)
+            if last:
+                pltpu.make_async_copy(
+                    grads.at[:, columns], grads_out.at[:, columns], grads_sem.at[index]
+                ).start()
+
+    learn(0, 0, 0, EXPERTS, first=True)
     for step in range(EXPERTS):
         across[step].wait_recv()
         further[step].start()
-        if step == EXPERTS - 3:
-            for index in range(EXPERTS // 2):
-                dacross[index].start()
-            for other in range(1, EXPERTS):
-                dnear[other].start()
+    for index in range(EXPERTS // 2):
+        dacross[index].start()
+    for step in range(1, EXPERTS):
+        dnear[step].start()
     for step in range(EXPERTS):
         beside[step].wait_recv()
-    learn(1, 0, False)
+    learn(1, 0, 0, EXPERTS)
+    learn(0, 1, 0, EXPERTS)
     for index in range(EXPERTS // 2):
         dacross[index].wait_recv()
         dbeside[index].start()
-    learn(0, 1, False)
-    for step in range(EXPERTS):
+    for step in range(EXPERTS // 2):
         further[step].wait_recv()
-    learn(1, 1, False)
+    learn(1, 1, 0, EXPERTS // 2)
+    for step in range(EXPERTS // 2, EXPERTS):
+        further[step].wait_recv()
+    learn(1, 1, EXPERTS // 2, EXPERTS // 2, last=True)
     for step in range(1, EXPERTS):
         dnear[step].wait_recv()
     for index in range(EXPERTS // 2):
@@ -434,6 +488,14 @@
         ).wait_recv()
     leave = pltpu.make_async_copy(drows, drows_out, out_sem)
     leave.start()
+
+    @pl.loop(0, width // tile)
+    def _(index):
+        columns = pl.ds(pl.multiple_of(index * tile, tile), tile)
+        pltpu.make_async_copy(
+            grads.at[:, columns], grads_out.at[:, columns], grads_sem.at[index]
+        ).wait()
+
     leave.wait()
     for step in range(EXPERTS):
         across[step].wait_send()
@@ -449,9 +511,10 @@
 
 def decode_kernel(
     groups,
+    step_rows,
     drows,
     roll,
-    dsel,
+    droutes,
     dscale,
     out,
     pre,
@@ -547,14 +610,32 @@
         copy.wait_recv()
     total = (back_in[0].astype(jnp.float32) + back_in[1].astype(jnp.float32)).astype(jnp.bfloat16)
     total = total.reshape(EXPERTS * slots, out_width)
+    ids = droutes[...]
+    turned = jnp.where(ids < expert, ids + EXPERTS - expert, ids - expert)
+    back_sel = one_hot_rows(EXPERTS * slots, decode_place(ids, step_rows, slots, turned))
     picked = lax.dot_general(
-        dsel[...], total, CONTRACT_MAJOR, preferred_element_type=jnp.float32
-    )
-    out[...] = (dscale[...] * picked).astype(jnp.bfloat16)
+        back_sel, total, CONTRACT_MAJOR, preferred_element_type=jnp.float32
+    )
+    out[...] = (as_column(dscale[...]) * picked).astype(jnp.bfloat16)
     for copy in back.values():
         copy.wait_send()
     for copy in side:
         copy.wait_send()
+
+
+def adam_kernel(grads, master, first, second, new_master, new_first, new_second, roll):
+    grad = grads[...]
+    moment = beta_one * first[...] + (1.0 - beta_one) * grad
+    square = beta_two * second[...] + (1.0 - beta_two) * grad * grad
+    correct_one = 1.0 - beta_one**step_count
+    correct_two = 1.0 - beta_two**step_count
+    held = master[...]
+    update = moment / correct_one / (jnp.sqrt(square / correct_two) + adam_eps)
+    value = held - adam_lr * (update + decay_rate * held)
+    new_first[...] = moment
+    new_second[...] = square
+    new_master[...] = value
+    roll[...] = value.astype(jnp.bfloat16)
 
 
 def moved_rows(
@@ -574,34 +655,26 @@
     hidden = master.shape[1]
     steps, dec_here = dec_tokens.shape[:2]
     slots = steps * DCAP
-    own_expert = lax.rem(lax.axis_index("group"), EXPERTS)
-    route_ids = routes[:, 0]
-    position = route_ids * (2 * CAP) + rank_within(route_ids, EXPERTS, 0)
-    position = jnp.concatenate([position, position + CAP])
-    sel = (
-        jnp.arange(EXPERTS * 2 * CAP, dtype=jnp.int32)[:, None] == position[None, :]
-    ).astype(jnp.bfloat16)
-    dec_ids = dec_routes[..., 0]
-    within = rank_within(dec_ids, EXPERTS, 1) + DCAP * jnp.arange(steps, dtype=jnp.int32)[:, None]
-    dec_place = jnp.arange(EXPERTS * slots, dtype=jnp.int32)[:, None]
-    dsel = (dec_place == (dec_ids * slots + within).reshape(1, -1)).astype(jnp.bfloat16)
-    turned = lax.rem(dec_ids + EXPERTS - own_expert, EXPERTS)
-    back_sel = (dec_place == (turned * slots + within).reshape(1, -1)).astype(jnp.bfloat16)
-
+    tokens_here = tokens.shape[0]
+    dec_line = dec_routes.reshape(1, steps * dec_here)
     master_rows = master[0]
     vmem = pl.BlockSpec(memory_space=pltpu.VMEM)
     anywhere = pl.BlockSpec(memory_space=pl.ANY)
     dma = pltpu.SemaphoreType.DMA
     rows_all = 2 * 2 * EXPERTS * 2 * CAP
     grads, drows = pl.pallas_call(
-        functools.partial(learner_kernel, groups),
+        functools.partial(learner_kernel, groups, dec_here),
         out_shape=(
             jax.ShapeDtypeStruct((3 * hidden, width), jnp.float32),
             jax.ShapeDtypeStruct((2, EXPERTS, slots, width), jnp.bfloat16),
         ),
         in_specs=[vmem] * 6 + [anywhere],
-        out_specs=(vmem, anywhere),
+        out_specs=(anywhere, anywhere),
         scratch_shapes=[
+            pltpu.VMEM((3 * hidden, width), jnp.float32),
+            pltpu.VMEM((tokens_here, 1), jnp.float32),
+            pltpu.VMEM((EXPERTS * 2 * CAP, 2 * tokens_here), jnp.bfloat16),
+            pltpu.VMEM((EXPERTS * slots, steps * dec_here), jnp.bfloat16),
             pltpu.VMEM((EXPERTS, 2 * CAP, width), jnp.bfloat16),
             pltpu.VMEM((2, 2, EXPERTS, 2 * CAP, width), jnp.bfloat16),
             pltpu.VMEM((EXPERTS, slots, width), jnp.bfloat16),
@@ -622,6 +695,7 @@
             dma((EXPERTS // 2,)),
             dma((EXPERTS // 2,)),
             dma(()),
+            dma((width // pick_tile(width),)),
         ],
         compiler_params=pltpu.CompilerParams(
             collective_id=0, has_side_effects=True, vmem_limit_bytes=56 * 2**20
@@ -635,27 +709,40 @@
     )(
         tokens,
         cotangent,
-        gate_scale,
-        sel,
+        gate_scale.reshape(1, tokens_here),
+        routes.reshape(1, tokens_here),
         dec_tokens.reshape(steps * dec_here, width),
-        dsel,
+        dec_line,
         master_rows,
     )
-    grads = jnp.concatenate(
-        [grads[part * hidden : (part + 1) * hidden] for part in range(3)], 1
-    )
-    moment_new = beta_one * moment_one[0] + (1.0 - beta_one) * grads
-    second_new = beta_two * moment_two[0] + (1.0 - beta_two) * grads * grads
-    correct_one = 1.0 - beta_one**step_count
-    correct_two = 1.0 - beta_two**step_count
-    update = moment_new / correct_one / (jnp.sqrt(second_new / correct_two) + adam_eps)
-    master_new = master_rows - adam_lr * (update + decay_rate * master_rows)
-    rollout = master_new.astype(jnp.bfloat16)
+    lines = min(32, hidden)
+    tall = hidden // lines
+    block = pl.BlockSpec((lines, width), lambda line, part: (line, part))
+    wide = jax.ShapeDtypeStruct((hidden, 3 * width), jnp.float32)
+    master_new, moment_new, second_new, rollout = pl.pallas_call(
+        adam_kernel,
+        grid=(tall, 3),
+        out_shape=(wide, wide, wide, jax.ShapeDtypeStruct(wide.shape, jnp.bfloat16)),
+        in_specs=[
+            pl.BlockSpec((lines, width), lambda line, part: (part * tall + line, 0)),
+            block,
+            block,
+            block,
+        ],
+        out_specs=(block, block, block, block),
+        compiler_params=pltpu.CompilerParams(vmem_limit_bytes=40 * 2**20),
+        cost_estimate=pl.CostEstimate(
+            flops=60 * hidden * width,
+            bytes_accessed=90 * hidden * width,
+            transcendentals=6 * hidden * width,
+        ),
+        name="adam",
+    )(grads, master_rows, moment_one[0], moment_two[0])
     out_width = width // 2
     rows_dec = 2 * EXPERTS * slots
-    pieces = 4
+    pieces = 8
     dec_out = pl.pallas_call(
-        functools.partial(decode_kernel, groups),
+        functools.partial(decode_kernel, groups, dec_here),
         out_shape=jax.ShapeDtypeStruct((steps * dec_here, out_width), jnp.bfloat16),
         in_specs=[vmem] * 4,
         out_specs=vmem,
@@ -683,8 +770,8 @@
     )(
         drows.reshape(rows_dec, width),
         rollout,
-        back_sel,
-        dec_scale.reshape(steps * dec_here, 1),
+        dec_line,
+        dec_scale.reshape(1, steps * dec_here),
     )
     return (
         master_new[None],

time: 277 us -> 246 us (0.89)
  other arithmetic: 48.7 us -> 1.99 us
  Pallas kernels: 208 us -> 235 us
  local copies, waits for them, and re-layouts: 17.7 us -> 7.36 us
    sub x2 -> x0, other arithmetic: 28.1 us -> none  [the longest x1 27.4 us: moved_rows(): master_new = master_rows - adam_lr * (update + decay_rate * master_rows)]
    pallas_call x2 -> x3, Pallas kernels: 208 us -> 235 us  [the longest x1 165 us: moved_rows(): pl.pallas_call(functools.partial(learner_kernel, groups, dec_here), out_s...]
    convert_element_type x5 -> x0, other arithmetic: 16.6 us -> none  [the longest x1 13.7 us: moved_rows(): rollout = master_new.astype(jnp.bfloat16)]
    slice x1 -> x0, local copies, waits for them, and re-layouts: 13.7 us -> none  [moved_rows(): grads[part * hidden:(part + 1) * hidden]]
    unnamed x7 -> x13, local copies, waits for them, and re-layouts: 3.69 us -> 6.68 us
where the time goes in v2:
time: 246 us; the launch traced here: 245 us
  Pallas kernels  235 us (96%)
  local copies, waits for them, and re-layouts  7.36 us (3%)
    pallas_call x1, Pallas kernels, moved_rows(): pl.pallas_call(functools.partial(learner_kernel, groups, dec_here), out_s...  165 us
    pallas_call x1, Pallas kernels, moved_rows(): pl.pallas_call(functools.partial(decode_kernel, groups, dec_here), out_sh...  36.2 us
    pallas_call x1, Pallas kernels, moved_rows(): pl.pallas_call(adam_kernel, grid=(tall, 3), out_shape=(wide, wide, wide,...  33 us
    unnamed x13, local copies, waits for them, and re-layouts  6.68 us

profile of v2, /device:TPU:0, one launch (start us, length us, event | category | flops | bytes accessed | tf_op | source)
XLA Modules:
  0.0 244.6 jit_solution(287555062551611904)
XLA Ops:
  0.6 0.5 broadcast.6
  1.1 1.3 reduce.6
  2.5 0.6 reshape.32.droutes
  3.1 165.4 %learner.1 = (f32[768,3584]{1,0:T(8,128)}, bf16[2,8,16,3584]{3,2,1,0:T(8,128)(2,1)}) custom-call(bf16[128,3584]{1,0:T(8,128)(2,1)} %tok.1, bf16[128,3584]{1,0:T(8,128)(2,1)} %cot.1, f32[1,128]{1,0:T(1,128)} %bitcast.23, s32[1,128]{1,0:T(1,128)} %bitcast.24, bf16[64,3584]{1,0:T(8,128)(2,1)} %bitcast.22, s32[1,64]{1,0:T(1,128)} %reshape.32.droutes, ...), custom_call_target="tpu_custom_call" | custom-call | flops 16911433728 | bytes 22020096 | tf_op jit(solution)/shard_map/learner/pallas_call | solution.py:665
  168.5 0.0 copy-start.4
  168.5 0.0 copy-start.2
  168.5 0.0 copy-start.3
  168.6 33.0 %adam.1 = (f32[256,10752]{1,0:T(8,128)}, f32[256,10752]{1,0:T(8,128)}, f32[256,10752]{1,0:T(8,128)}, bf16[256,10752]{1,0:T(8,128)(2,1)S(1)}) custom-call(f32[768,3584]{1,0:T(8,128)} %get-tuple-element.10.grads, f32[256,10752]{1,0:T(8,128)} %bitcast.16, f32[256,10752]{1,0:T(8,128)} %bitcast.17, f32[256,10752]{1,0:T(8,128)} %bitcast.18), custom_call_target="tpu_custom_call" | custom-call | flops 55050240 | bytes 82575360 | tf_op jit(solution)/shard_map/adam/pallas_call | solution.py:722
  201.6 0.0 copy-start
  201.6 2.4 copy-done
  204.0 0.5 broadcast.7
  204.5 0.0 copy-done.4
  204.5 0.6 reduce.7
  205.1 0.1 reshape.34.dscale
  205.2 0.0 copy-done.2
  205.2 0.0 copy-done.3
  205.2 0.0 copy-start.1
  205.2 2.6 %copy-done.1 = bf16[256,10752]{1,0:T(8,128)(2,1)S(1)} copy-done((bf16[256,10752]{1,0:T(8,128)(2,1)S(1)}, bf16[256,10752]{1,0:T(8,128)(2,1)}, u32[]{:S(2)}) %copy-start.1) | copy-done | bytes 5505048
  207.8 36.2 %decode.1 = bf16[64,1792]{1,0:T(8,128)(2,1)S(1)} custom-call(bf16[256,3584]{1,0:T(8,128)(2,1)S(1)} %bitcast.13, bf16[256,10752]{1,0:T(8,128)(2,1)S(1)} %copy-done.1, s32[1,64]{1,0:T(1,128)S(1)} %copy-done.3, f32[1,64]{1,0:T(1,128)S(1)} %reshape.34.dscale), custom_call_target="tpu_custom_call" | custom-call | flops 1409286144 | bytes 5505024 | tf_op jit(solution)/shard_map/decode/pallas_call | solution.py:744
  243.9 0.7 copy.15
Async XLA Ops:
  168.5 36.0 %copy-start.4 = (f32[4,16,1]{1,2,0:T(1,128)S(1)}, f32[4,16,1]{1,2,0:T(1,128)}, u32[]{:S(2)}) copy-start(f32[4,16,1]{1,2,0:T(1,128)} %param.19) | copy-start | bytes 772
  168.5 36.7 %copy-start.2 = (bf16[2,8,16,3584]{3,2,1,0:T(8,128)(2,1)S(1)}, bf16[2,8,16,3584]{3,2,1,0:T(8,128)(2,1)}, u32[]{:S(2)}) copy-start(bf16[2,8,16,3584]{3,2,1,0:T(8,128)(2,1)} %get-tuple-element.14) | copy-start | bytes 5505028
  168.5 36.7 %copy-start.3 = (s32[1,64]{1,0:T(1,128)S(1)}, s32[1,64]{1,0:T(1,128)}, u32[]{:S(2)}) copy-start(s32[1,64]{1,0:T(1,128)} %reshape.32.droutes) | copy-start | bytes 772
  201.6 2.4 copy-start
  205.2 2.6 %copy-start.1 = (bf16[256,10752]{1,0:T(8,128)(2,1)S(1)}, bf16[256,10752]{1,0:T(8,128)(2,1)}, u32[]{:S(2)}) copy-start(bf16[256,10752]{1,0:T(8,128)(2,1)} %copy-done) | copy-start | bytes 16515076

commit v3 on v2

--- a/solution.py
+++ b/solution.py
@@ -165,6 +165,7 @@
 
 
 MESH = pl.DeviceIdType.MESH
+PIECES = 4
 CONTRACT_MINOR = (((1,), (1,)), ((), ()))
 CONTRACT_MAJOR = (((0,), (0,)), ((), ()))
 
@@ -218,7 +219,10 @@
     pl.semaphore_signal(
         barrier, inc=1, device_id={"group": own_group, "dp": 1 - own_dp}, device_id_type=MESH
     )
-    pl.semaphore_wait(barrier, groups)
+
+
+def await_peers(groups):
+    pl.semaphore_wait(pltpu.get_barrier_semaphore(), groups)
 
 
 def learner_kernel(
@@ -234,28 +238,39 @@
     grads_out,
     drows_out,
     grads,
+    rounded,
     gate_scale,
     sel,
+    far_sel,
     dsel,
+    raw,
+    far_raw,
+    ids_out,
+    ids_in,
     packed,
+    far_packed,
     rows,
     dpacked,
     drows,
     weights,
     pre,
     left,
+    raw_send,
+    raw_recv,
+    ids_send,
+    ids_recv,
     near_send,
     near_recv,
-    half_send,
-    half_recv,
+    far_send,
+    far_recv,
     side_send,
     side_recv,
+    far_side_send,
+    far_side_recv,
     dnear_send,
     dnear_recv,
     dhalf_send,
     dhalf_recv,
-    dside_send,
-    dside_recv,
     out_sem,
     grads_sem,
 ):
@@ -263,11 +278,13 @@
     dp = lax.axis_index("dp")
     half = group // EXPERTS
     expert = lax.rem(group, EXPERTS)
-    width = tok.shape[1]
+    count, width = tok.shape
     hidden = weights.shape[0]
     tile = pick_tile(width)
     block = 2 * CAP
     chunk = EXPERTS * block
+    piece = width // PIECES
+    spans = [pl.ds(index * piece, piece) for index in range(PIECES)]
 
     def remote(src, dst, send, recv, to_group, to_dp):
         return pltpu.make_async_remote_copy(
@@ -279,25 +296,52 @@
             device_id_type=MESH,
         )
 
+    def slots_of(ids):
+        place = (ids * block).astype(jnp.float32) + count_before(ids, count)
+        return one_hot_rows(chunk, jnp.concatenate([place, place + CAP], 1))
+
+    greet_peers(group, dp, groups)
     gate_scale[...] = as_column(scale_line[...])
-    ids = routes[...]
-    place = (ids * block).astype(jnp.float32) + count_before(ids, ids.shape[1])
-    sel[...] = one_hot_rows(chunk, jnp.concatenate([place, place + CAP], 1))
-    slots = dpacked.shape[1]
-    ids = droutes[...]
-    dsel[...] = one_hot_rows(EXPERTS * slots, decode_place(ids, step_rows, slots, ids))
+    ids_out[...] = jnp.broadcast_to(routes[...].astype(jnp.float32), ids_out.shape).astype(
+        jnp.bfloat16
+    )
+    raw[:count] = tok[...]
 
     @pl.loop(0, width // tile)
     def _(index):
         columns = pl.ds(pl.multiple_of(index * tile, tile), tile)
-        scaled = (gate_scale[...] * cot[:, columns].astype(jnp.float32)).astype(jnp.bfloat16)
-        both = jnp.concatenate([tok[:, columns], scaled], 0)
-        picked = jnp.dot(sel[...], both, preferred_element_type=jnp.float32).astype(jnp.bfloat16)
-        packed[:, :, columns] = picked.reshape(EXPERTS, block, tile)
-        picked = jnp.dot(dsel[...], dtok[:, columns], preferred_element_type=jnp.float32)
-        dpacked[:, :, columns] = picked.astype(jnp.bfloat16).reshape(EXPERTS, -1, tile)
-
-    greet_peers(group, dp, groups)
+        raw[count:, columns] = (gate_scale[...] * cot[:, columns].astype(jnp.float32)).astype(
+            jnp.bfloat16
+        )
+
+    await_peers(groups)
+    other_group = (1 - half) * EXPERTS + expert
+    ids_copy = remote(ids_out, ids_in, ids_send, ids_recv, other_group, dp)
+    ids_copy.start()
+    across = [
+        remote(
+            raw.at[:, spans[index]],
+            far_raw.at[:, spans[index]],
+            raw_send.at[index],
+            raw_recv.at[index],
+            other_group,
+            dp,
+        )
+        for index in range(PIECES)
+    ]
+    for copy in across:
+        copy.start()
+
+    sel[...] = slots_of(routes[...])
+
+    @pl.loop(0, width // tile)
+    def _(index):
+        columns = pl.ds(pl.multiple_of(index * tile, tile), tile)
+        picked = jnp.dot(sel[...], raw[:, columns], preferred_element_type=jnp.float32)
+        packed[:, :, columns] = picked.astype(jnp.bfloat16).reshape(EXPERTS, block, tile)
+
+    def peer(step):
+        return half * EXPERTS + lax.rem(expert + step, EXPERTS)
 
     near = [None] + [
         remote(
@@ -305,90 +349,82 @@
             rows.at[0, 0, step],
             near_send.at[step],
             near_recv.at[step],
-            half * EXPERTS + lax.rem(expert + step, EXPERTS),
+            peer(step),
             dp,
         )
         for step in range(1, EXPERTS)
     ]
-    other_group = (1 - half) * EXPERTS + expert
-    across = []
-    beside = []
-    for step in range(EXPERTS):
-        source = packed.at[expert] if step == 0 else rows.at[0, 0, step]
-        across.append(
-            remote(
-                source,
-                rows.at[0, 1, step],
-                half_send.at[step],
-                half_recv.at[step],
-                other_group,
-                dp,
-            )
-        )
-        beside.append(
-            remote(
-                source,
-                rows.at[1, 0, step],
-                side_send.at[0, step],
-                side_recv.at[0, step],
+    beside = [
+        remote(
+            packed.at[expert] if step == 0 else rows.at[0, 0, step],
+            rows.at[1, 0, step],
+            side_send.at[step],
+            side_recv.at[step],
+            group,
+            1 - dp,
+        )
+        for step in range(EXPERTS)
+    ]
+    far_near = {}
+    further = {}
+    for index in range(PIECES):
+        for step in range(EXPERTS):
+            if step:
+                far_near[index, step] = remote(
+                    far_packed.at[lax.rem(expert + step, EXPERTS), :, spans[index]],
+                    rows.at[0, 1, step, :, spans[index]],
+                    far_send.at[index, step],
+                    far_recv.at[index, step],
+                    peer(step),
+                    dp,
+                )
+            further[index, step] = remote(
+                rows.at[0, 1, step, :, spans[index]],
+                rows.at[1, 1, step, :, spans[index]],
+                far_side_send.at[index, step],
+                far_side_recv.at[index, step],
                 group,
                 1 - dp,
             )
-        )
-    further = [
-        remote(
-            rows.at[0, 1, step],
-            rows.at[1, 1, step],
-            side_send.at[1, step],
-            side_recv.at[1, step],
-            group,
-            1 - dp,
-        )
-        for step in range(EXPERTS)
-    ]
     dnear = [None] + [
         remote(
             dpacked.at[lax.rem(expert + step, EXPERTS)],
             drows.at[0, step],
             dnear_send.at[step],
             dnear_recv.at[step],
-            half * EXPERTS + lax.rem(expert + step, EXPERTS),
+            peer(step),
             dp,
         )
         for step in range(1, EXPERTS)
     ]
-    dacross = []
-    dbeside = []
-    for index in range(EXPERTS // 2):
-        step = 2 * index + dp
-        dacross.append(
-            remote(
-                dpacked.at[lax.rem(expert + step, EXPERTS)],
-                drows.at[1, step],
-                dhalf_send.at[index],
-                dhalf_recv.at[index],
-                (1 - half) * EXPERTS + lax.rem(expert + step, EXPERTS),
-                dp,
-            )
-        )
-        dbeside.append(
-            remote(
-                drows.at[1, step],
-                drows.at[1, step],
-                dside_send.at[index],
-                dside_recv.at[index],
-                group,
-                1 - dp,
-            )
-        )
-
-    across[0].start()
+    dacross = [
+        remote(
+            dpacked.at[lax.rem(expert + step, EXPERTS)],
+            drows.at[1, step],
+            dhalf_send.at[step],
+            dhalf_recv.at[step],
+            (1 - half) * EXPERTS + lax.rem(expert + step, EXPERTS),
+            dp,
+        )
+        for step in range(EXPERTS)
+    ]
+
     beside[0].start()
     for step in range(1, EXPERTS):
         near[step].start()
     rows[0, 0, 0] = packed[expert]
+
+    slots = dpacked.shape[1]
+    ids = droutes[...]
+    dsel[...] = one_hot_rows(EXPERTS * slots, decode_place(ids, step_rows, slots, ids))
+
+    @pl.loop(0, width // tile)
+    def _(index):
+        columns = pl.ds(pl.multiple_of(index * tile, tile), tile)
+        picked = jnp.dot(dsel[...], dtok[:, columns], preferred_element_type=jnp.float32)
+        dpacked[:, :, columns] = picked.astype(jnp.bfloat16).reshape(EXPERTS, -1, tile)
+
     drows[0, 0] = dpacked[expert]
-
     lines = min(16, hidden)
 
     def cast_body(source):
@@ -404,28 +440,27 @@
 
     for step in range(1, EXPERTS):
         near[step].wait_recv()
-        across[step].start()
         beside[step].start()
 
-    def learn(side, far, begin_step, steps, first=False, last=False):
-        own = rows.at[side, far, pl.ds(begin_step, steps)]
-        height = steps * block
-        pre[:height] = jnp.zeros((height, 3 * hidden), jnp.float32)
+    def score(own, start, size):
+        operand = own[:, :, pl.ds(start, size)].reshape(chunk, size)
+        for part in range(3):
+            pre[:, part * hidden : (part + 1) * hidden] += lax.dot_general(
+                operand,
+                weights[:, pl.ds(pl.multiple_of(part * width + start, 128), size)],
+                CONTRACT_MINOR,
+                preferred_element_type=jnp.float32,
+            )
+
+    def score_all(own):
+        pre[...] = jnp.zeros_like(pre)
 
         @pl.loop(0, width // tile)
         def _(index):
-            start = pl.multiple_of(index * tile, tile)
-            operand = own[:, :, pl.ds(start, tile)].reshape(height, tile)
-            for part in range(3):
-                begin = pl.multiple_of(part * width + start, 128)
-                pre[:height, part * hidden : (part + 1) * hidden] += lax.dot_general(
-                    operand,
-                    weights[:, pl.ds(begin, tile)],
-                    CONTRACT_MINOR,
-                    preferred_element_type=jnp.float32,
-                )
-
-        parts = pre[:height].reshape(steps, block, 3 * hidden)
+            score(own, pl.multiple_of(index * tile, tile), tile)
+
+    def accumulate(own, first=False, last=False):
+        parts = pre[...].reshape(EXPERTS, block, 3 * hidden)
         gate_pre = parts[:, :CAP, :hidden]
         up_pre = parts[:, :CAP, hidden : 2 * hidden]
         back_pre = parts[:, CAP:, 2 * hidden :]
@@ -433,59 +468,81 @@
         zeros = jnp.zeros_like(gate_pre)
         top = jnp.concatenate([back_pre * up_pre * silu_grad, back_pre * silu_val, zeros], 2)
         bottom = jnp.concatenate([zeros, zeros, silu_val * up_pre], 2)
-        left[:, :height] = (
+        left[...] = (
             jnp.concatenate([top, bottom], 1)
-            .reshape(height, 3 * hidden)
+            .reshape(chunk, 3 * hidden)
             .T.astype(jnp.bfloat16)
         )
 
         @pl.loop(0, width // tile)
         def _(index):
             columns = pl.ds(pl.multiple_of(index * tile, tile), tile)
-            operand = own[:, :, columns].reshape(height, tile)
-            value = jnp.dot(left[:, :height], operand, preferred_element_type=jnp.float32)
+            operand = own[:, :, columns].reshape(chunk, tile)
+            value = jnp.dot(left[...], operand, preferred_element_type=jnp.float32)
             if first:
                 grads[:, columns] = value
+            elif last:
+                rounded[:, columns] = (grads[:, columns] + value).astype(jnp.bfloat16)
+                pltpu.make_async_copy(
+                    rounded.at[:, columns], grads_out.at[:, columns], grads_sem.at[index]
+                ).start()
             else:
                 grads[:, columns] += value
-            if last:
-                pltpu.make_async_copy(
-                    grads.at[:, columns], grads_out.at[:, columns], grads_sem.at[index]
-                ).start()
-
-    learn(0, 0, 0, EXPERTS, first=True)
+
+    def spread(index):
+        across[index].wait_recv()
+        if index == 0:
+            ids_copy.wait_recv()
+            far_sel[...] = slots_of(ids_in[0:1, :].astype(jnp.float32).astype(jnp.int32))
+        picked = jnp.dot(
+            far_sel[...], far_raw[:, spans[index]], preferred_element_type=jnp.float32
+        )
+        far_packed[:, :, spans[index]] = picked.astype(jnp.bfloat16).reshape(
+            EXPERTS, block, piece
+        )
+        for step in range(1, EXPERTS):
+            far_near[index, step].start()
+        rows[0, 1, 0, :, spans[index]] = far_packed[expert, :, spans[index]]
+        further[index, 0].start()
+
+    def pass_on(index):
+        for step in range(1, EXPERTS):
+            far_near[index, step].wait_recv()
+            further[index, step].start()
+
+    spread(0)
+    own = rows.at[0, 0]
+    score_all(own)
+    accumulate(own, first=True)
+    pass_on(0)
+    for index in range(1, PIECES):
+        spread(index)
+        if index == PIECES - 1:
+            for step in range(EXPERTS):
+                dacross[step].start()
+            for step in range(1, EXPERTS):
+                dnear[step].start()
+        pass_on(index)
+        if index == PIECES - 2:
+            for step in range(EXPERTS):
+                beside[step].wait_recv()
+            own = rows.at[1, 0]
+            score_all(own)
+            accumulate(own)
+    own = rows.at[0, 1]
+    score_all(own)
+    accumulate(own)
+    own = rows.at[1, 1]
+    pre[...] = jnp.zeros_like(pre)
+    for index in range(PIECES):
+        for step in range(EXPERTS):
+            further[index, step].wait_recv()
+        score(own, index * piece, piece)
+    accumulate(own, last=True)
     for step in range(EXPERTS):
-        across[step].wait_recv()
-        further[step].start()
-    for index in range(EXPERTS // 2):
-        dacross[index].start()
-    for step in range(1, EXPERTS):
-        dnear[step].start()
-    for step in range(EXPERTS):
-        beside[step].wait_recv()
-    learn(1, 0, 0, EXPERTS)
-    learn(0, 1, 0, EXPERTS)
-    for index in range(EXPERTS // 2):
-        dacross[index].wait_recv()
-        dbeside[index].start()
-    for step in range(EXPERTS // 2):
-        further[step].wait_recv()
-    learn(1, 1, 0, EXPERTS // 2)
-    for step in range(EXPERTS // 2, EXPERTS):
-        further[step].wait_recv()
-    learn(1, 1, EXPERTS // 2, EXPERTS // 2, last=True)
-    for step in range(1, EXPERTS):
-        dnear[step].wait_recv()
-    for index in range(EXPERTS // 2):
-        step = 2 * index + 1 - dp
-        remote(
-            drows.at[1, step],
-            drows.at[1, step],
-            dside_send.at[index],
-            dside_recv.at[index],
-            group,
-            1 - dp,
-        ).wait_recv()
+        dacross[step].wait_recv()
+        if step:
+            dnear[step].wait_recv()
     leave = pltpu.make_async_copy(drows, drows_out, out_sem)
     leave.start()
 
@@ -493,30 +550,29 @@
     def _(index):
         columns = pl.ds(pl.multiple_of(index * tile, tile), tile)
         pltpu.make_async_copy(
-            grads.at[:, columns], grads_out.at[:, columns], grads_sem.at[index]
+            rounded.at[:, columns], grads_out.at[:, columns], grads_sem.at[index]
         ).wait()
 
     leave.wait()
-    for step in range(EXPERTS):
-        across[step].wait_send()
-        beside[step].wait_send()
-        further[step].wait_send()
-        if step:
-            near[step].wait_send()
-            dnear[step].wait_send()
-    for index in range(EXPERTS // 2):
-        dacross[index].wait_send()
-        dbeside[index].wait_send()
+    ids_copy.wait_send()
+    for copy in across + beside + near[1:] + dnear[1:] + dacross:
+        copy.wait_send()
+    for copy in far_near.values():
+        copy.wait_send()
+    for copy in further.values():
+        copy.wait_send()
 
 
 def decode_kernel(
     groups,
     step_rows,
-    drows,
-    roll,
+    drows_in,
+    roll_in,
     droutes,
     dscale,
     out,
+    drows,
+    roll,
     pre,
     own,
     side_out,
@@ -527,6 +583,7 @@
     side_recv,
     back_send,
     back_recv,
+    in_sem,
 ):
     group = lax.axis_index("group")
     dp = lax.axis_index("dp")
@@ -539,8 +596,21 @@
     slots = drows.shape[0] // (2 * EXPERTS)
     pieces = side_out.shape[0]
     per_piece = 2 * EXPERTS // pieces
+    fetches = [
+        pltpu.make_async_copy(drows_in, drows, in_sem.at[0]),
+        pltpu.make_async_copy(
+            roll_in.at[:, : 2 * width], roll.at[:, : 2 * width], in_sem.at[1]
+        ),
+        pltpu.make_async_copy(
+            roll_in.at[:, 2 * width :], roll.at[:, 2 * width :], in_sem.at[2]
+        ),
+    ]
+    for fetch in fetches:
+        fetch.start()
     greet_peers(group, dp, groups)
     pre[...] = jnp.zeros_like(pre)
+    fetches[0].wait()
+    fetches[1].wait()
 
     @pl.loop(0, width // tile)
     def _(index):
@@ -557,6 +627,7 @@
 
     dec_silu, unused_grad = silu_parts(pre[:, :hidden])
     act = (dec_silu * pre[:, hidden:]).astype(jnp.bfloat16)
+    fetches[2].wait()
     strip = 256 if out_width % 256 == 0 else 128
     for index in range(out_width // strip):
         begin = pl.multiple_of(2 * width + (1 - dp) * out_width + index * strip, 128)
@@ -576,6 +647,7 @@
         )
         for piece in range(pieces)
     ]
+    await_peers(groups)
     for piece in order:
         side[piece].start()
     for index in range(out_width // strip):
@@ -624,14 +696,14 @@
 
 
 def adam_kernel(grads, master, first, second, new_master, new_first, new_second, roll):
-    grad = grads[...]
+    grad = grads[...].astype(jnp.float32)
     moment = beta_one * first[...] + (1.0 - beta_one) * grad
     square = beta_two * second[...] + (1.0 - beta_two) * grad * grad
-    correct_one = 1.0 - beta_one**step_count
-    correct_two = 1.0 - beta_two**step_count
-    held = master[...]
-    update = moment / correct_one / (jnp.sqrt(square / correct_two) + adam_eps)
-    value = held - adam_lr * (update + decay_rate * held)
+    scale_one = adam_lr / (1.0 - beta_one**step_count)
+    scale_two = 1.0 / (1.0 - beta_two**step_count)
+    corrected = square * scale_two
+    root = corrected * lax.rsqrt(corrected) + adam_eps
+    value = (1.0 - adam_lr * decay_rate) * master[...] - (scale_one * moment) / root
     new_first[...] = moment
     new_second[...] = square
     new_master[...] = value
@@ -665,16 +737,23 @@
     grads, drows = pl.pallas_call(
         functools.partial(learner_kernel, groups, dec_here),
         out_shape=(
-            jax.ShapeDtypeStruct((3 * hidden, width), jnp.float32),
+            jax.ShapeDtypeStruct((3 * hidden, width), jnp.bfloat16),
             jax.ShapeDtypeStruct((2, EXPERTS, slots, width), jnp.bfloat16),
         ),
         in_specs=[vmem] * 6 + [anywhere],
         out_specs=(anywhere, anywhere),
         scratch_shapes=[
             pltpu.VMEM((3 * hidden, width), jnp.float32),
+            pltpu.VMEM((3 * hidden, width), jnp.bfloat16),
             pltpu.VMEM((tokens_here, 1), jnp.float32),
             pltpu.VMEM((EXPERTS * 2 * CAP, 2 * tokens_here), jnp.bfloat16),
+            pltpu.VMEM((EXPERTS * 2 * CAP, 2 * tokens_here), jnp.bfloat16),
             pltpu.VMEM((EXPERTS * slots, steps * dec_here), jnp.bfloat16),
+            pltpu.VMEM((2 * tokens_here, width), jnp.bfloat16),
+            pltpu.VMEM((2 * tokens_here, width), jnp.bfloat16),
+            pltpu.VMEM((16, tokens_here), jnp.bfloat16),
+            pltpu.VMEM((16, tokens_here), jnp.bfloat16),
+            pltpu.VMEM((EXPERTS, 2 * CAP, width), jnp.bfloat16),
             pltpu.VMEM((EXPERTS, 2 * CAP, width), jnp.bfloat16),
             pltpu.VMEM((2, 2, EXPERTS, 2 * CAP, width), jnp.bfloat16),
             pltpu.VMEM((EXPERTS, slots, width), jnp.bfloat16),
@@ -682,18 +761,22 @@
             pltpu.VMEM((hidden, 3 * width), jnp.bfloat16),
             pltpu.VMEM((EXPERTS * 2 * CAP, 3 * hidden), jnp.float32),
             pltpu.VMEM((3 * hidden, EXPERTS * 2 * CAP), jnp.bfloat16),
+            dma((PIECES,)),
+            dma((PIECES,)),
+            dma(()),
+            dma(()),
+            dma((EXPERTS,)),
+            dma((EXPERTS,)),
+            dma((PIECES, EXPERTS)),
+            dma((PIECES, EXPERTS)),
+            dma((EXPERTS,)),
+            dma((EXPERTS,)),
+            dma((PIECES, EXPERTS)),
+            dma((PIECES, EXPERTS)),
             dma((EXPERTS,)),
             dma((EXPERTS,)),
             dma((EXPERTS,)),
             dma((EXPERTS,)),
-            dma((2, EXPERTS)),
-            dma((2, EXPERTS)),
-            dma((EXPERTS,)),
-            dma((EXPERTS,)),
-            dma((EXPERTS // 2,)),
-            dma((EXPERTS // 2,)),
-            dma((EXPERTS // 2,)),
-            dma((EXPERTS // 2,)),
             dma(()),
             dma((width // pick_tile(width),)),
         ],
@@ -744,9 +827,11 @@
     dec_out = pl.pallas_call(
         functools.partial(decode_kernel, groups, dec_here),
         out_shape=jax.ShapeDtypeStruct((steps * dec_here, out_width), jnp.bfloat16),
-        in_specs=[vmem] * 4,
+        in_specs=[anywhere, anywhere, vmem, vmem],
         out_specs=vmem,
         scratch_shapes=[
+            pltpu.VMEM((rows_dec, width), jnp.bfloat16),
+            pltpu.VMEM((hidden, 3 * width), jnp.bfloat16),
             pltpu.VMEM((rows_dec, 2 * hidden), jnp.float32),
             pltpu.VMEM((pieces, rows_dec // pieces, out_width), jnp.float32),
             pltpu.VMEM((pieces, rows_dec // pieces, out_width), jnp.bfloat16),
@@ -757,9 +842,10 @@
             dma((pieces,)),
             dma((2, EXPERTS)),
             dma((2, EXPERTS)),
+            dma((3,)),
         ],
         compiler_params=pltpu.CompilerParams(
-            collective_id=1, has_side_effects=True, vmem_limit_bytes=40 * 2**20
+            collective_id=1, has_side_effects=True, vmem_limit_bytes=56 * 2**20
         ),
         cost_estimate=pl.CostEstimate(
             flops=6 * rows_dec * hidden * width,

time: 246 us -> 247 us (level)
    pallas_call x1, Pallas kernels: 33 us -> 29.1 us  [moved_rows(): pl.pallas_call(adam_kernel, grid=(tall, 3), out_shape=(wide, wide, wide,...]
    pallas_call x1, Pallas kernels: 165 us -> 168 us  [moved_rows(): pl.pallas_call(functools.partial(learner_kernel, groups, dec_here), out_s...]
    unnamed x13 -> x9, local copies, waits for them, and re-layouts: 6.68 us -> 7.69 us
where the time goes in v3:
time: 247 us; the launch traced here: 246 us
  Pallas kernels  235 us (95%)
  local copies, waits for them, and re-layouts  8.96 us (4%)
    pallas_call x1, Pallas kernels, moved_rows(): pl.pallas_call(functools.partial(learner_kernel, groups, dec_here), out_s...  168 us
    pallas_call x1, Pallas kernels, moved_rows(): pl.pallas_call(functools.partial(decode_kernel, groups, dec_here), out_sh...  37 us
    pallas_call x1, Pallas kernels, moved_rows(): pl.pallas_call(adam_kernel, grid=(tall, 3), out_shape=(wide, wide, wide,...  29.1 us
    unnamed x9, local copies, waits for them, and re-layouts  7.69 us

profile of v3, /device:TPU:0, one launch (start us, length us, event | category | flops | bytes accessed | tf_op | source)
XLA Modules:
  0.0 246.2 jit_solution(11377375146737533153)
XLA Ops:
  0.6 0.5 broadcast.6
  1.1 1.3 reduce.6
  2.5 0.6 reshape.32.droutes
  3.1 168.4 %learner.1 = (bf16[768,3584]{1,0:T(8,128)(2,1)}, bf16[2,8,16,3584]{3,2,1,0:T(8,128)(2,1)}) custom-call(bf16[128,3584]{1,0:T(8,128)(2,1)} %tok.1, bf16[128,3584]{1,0:T(8,128)(2,1)} %cot.1, f32[1,128]{1,0:T(1,128)} %bitcast.23, s32[1,128]{1,0:T(1,128)} %bitcast.24, bf16[64,3584]{1,0:T(8,128)(2,1)} %bitcast.22, s32[1,64]{1,0:T(1,128)} %reshape.32.droutes, ...), custom_call_target="tpu_custom_call" | custom-call | flops 16911433728 | bytes 22020096 | tf_op jit(solution)/shard_map/learner/pallas_call | solution.py:737
  171.5 0.0 copy-start
  171.5 2.6 %copy-done = bf16[768,3584]{1,0:T(8,128)(2,1)S(1)} copy-done((bf16[768,3584]{1,0:T(8,128)(2,1)S(1)}, bf16[768,3584]{1,0:T(8,128)(2,1)}, u32[]{:S(2)}) %copy-start) | copy-done | bytes 5505048
  174.1 0.0 copy-start.2
  174.1 29.1 %adam.1 = (f32[256,10752]{1,0:T(8,128)}, f32[256,10752]{1,0:T(8,128)}, f32[256,10752]{1,0:T(8,128)}, bf16[256,10752]{1,0:T(8,128)(2,1)S(1)}) custom-call(bf16[768,3584]{1,0:T(8,128)(2,1)S(1)} %copy-done, f32[256,10752]{1,0:T(8,128)} %bitcast.14, f32[256,10752]{1,0:T(8,128)} %bitcast.15, f32[256,10752]{1,0:T(8,128)} %bitcast.16), custom_call_target="tpu_custom_call" | custom-call | flops 55050240 | bytes 82575360 | tf_op jit(solution)/shard_map/adam/pallas_call | solution.py:805
  203.2 0.0 copy-start.1
  203.2 2.4 copy-done.1
  205.6 0.6 broadcast.7
  206.2 0.0 copy-done.2
  206.2 0.7 reduce.7
  206.9 0.7 reshape.34.dscale
  207.6 37.0 %decode.1 = bf16[64,1792]{1,0:T(8,128)(2,1)} custom-call(bf16[256,3584]{1,0:T(8,128)(2,1)} %bitcast.17, bf16[256,10752]{1,0:T(8,128)(2,1)} %copy-done.1, s32[1,64]{1,0:T(1,128)} %reshape.32.droutes, f32[1,64]{1,0:T(1,128)} %reshape.34.dscale), custom_call_target="tpu_custom_call" | custom-call | flops 1409286144 | bytes 5505024 | tf_op jit(solution)/shard_map/decode/pallas_call | solution.py:827
  244.6 1.6 copy.15
Async XLA Ops:
  171.5 2.6 %copy-start = (bf16[768,3584]{1,0:T(8,128)(2,1)S(1)}, bf16[768,3584]{1,0:T(8,128)(2,1)}, u32[]{:S(2)}) copy-start(bf16[768,3584]{1,0:T(8,128)(2,1)} %get-tuple-element.10.grads) | copy-start | bytes 16515076
  174.1 32.1 %copy-start.2 = (f32[4,16,1]{1,2,0:T(1,128)S(1)}, f32[4,16,1]{1,2,0:T(1,128)}, u32[]{:S(2)}) copy-start(f32[4,16,1]{1,2,0:T(1,128)} %param.19) | copy-start | bytes 772
  203.2 2.4 copy-start.1

commit v4 on v3

--- a/solution.py
+++ b/solution.py
@@ -189,6 +189,10 @@
     return jnp.sum(running * onehot, axis=0, keepdims=True)
 
 
+def in_line(ref):
+    return jnp.concatenate([ref[index] for index in range(ref.shape[0])], 1)
+
+
 def as_column(line):
     count = line.shape[1]
     across = lax.broadcasted_iota(jnp.int32, (count, count), 0)
@@ -219,10 +223,14 @@
     pl.semaphore_signal(
         barrier, inc=1, device_id={"group": own_group, "dp": 1 - own_dp}, device_id_type=MESH
     )
+    twin = own_group + 1 - 2 * lax.rem(own_group, 2)
+    pl.semaphore_signal(
+        barrier, inc=1, device_id={"group": twin, "dp": 1 - own_dp}, device_id_type=MESH
+    )
 
 
 def await_peers(groups):
-    pl.semaphore_wait(pltpu.get_barrier_semaphore(), groups)
+    pl.semaphore_wait(pltpu.get_barrier_semaphore(), groups + 1)
 
 
 def learner_kernel(
@@ -409,13 +417,23 @@
         for step in range(EXPERTS)
     ]
 
+    twin = jnp.where(lax.rem(expert, 2) == 0, 1, EXPERTS - 1)
+    mirror = EXPERTS - twin
     beside[0].start()
+    remote(
+        packed.at[lax.rem(expert + twin, EXPERTS)],
+        rows.at[1, 0, twin],
+        side_send.at[mirror],
+        side_recv.at[twin],
+        peer(twin),
+        1 - dp,
+    ).start()
     for step in range(1, EXPERTS):
         near[step].start()
     rows[0, 0, 0] = packed[expert]
 
     slots = dpacked.shape[1]
-    ids = droutes[...]
+    ids = in_line(droutes)
     dsel[...] = one_hot_rows(EXPERTS * slots, decode_place(ids, step_rows, slots, ids))
 
     @pl.loop(0, width // tile)
@@ -438,7 +456,17 @@
         out_specs=[],
     )(master)
 
-    for step in range(1, EXPERTS):
+    near[1].wait_recv()
+    near[EXPERTS - 1].wait_recv()
+    remote(
+        rows.at[0, 0, twin],
+        rows.at[1, 0, twin],
+        side_send.at[twin],
+        side_recv.at[twin],
+        group,
+        1 - dp,
+    ).start()
+    for step in range(2, EXPERTS - 1):
         near[step].wait_recv()
         beside[step].start()
 
@@ -682,13 +710,13 @@
         copy.wait_recv()
     total = (back_in[0].astype(jnp.float32) + back_in[1].astype(jnp.float32)).astype(jnp.bfloat16)
     total = total.reshape(EXPERTS * slots, out_width)
-    ids = droutes[...]
+    ids = in_line(droutes)
     turned = jnp.where(ids < expert, ids + EXPERTS - expert, ids - expert)
     back_sel = one_hot_rows(EXPERTS * slots, decode_place(ids, step_rows, slots, turned))
     picked = lax.dot_general(
         back_sel, total, CONTRACT_MAJOR, preferred_element_type=jnp.float32
     )
-    out[...] = (as_column(dscale[...]) * picked).astype(jnp.bfloat16)
+    out[...] = (as_column(in_line(dscale)) * picked).astype(jnp.bfloat16)
     for copy in back.values():
         copy.wait_send()
     for copy in side:
@@ -728,7 +756,7 @@
     steps, dec_here = dec_tokens.shape[:2]
     slots = steps * DCAP
     tokens_here = tokens.shape[0]
-    dec_line = dec_routes.reshape(1, steps * dec_here)
+    dec_line = jnp.transpose(dec_routes, (0, 2, 1))
     master_rows = master[0]
     vmem = pl.BlockSpec(memory_space=pltpu.VMEM)
     anywhere = pl.BlockSpec(memory_space=pl.ANY)
@@ -813,7 +841,7 @@
             block,
         ],
         out_specs=(block, block, block, block),
-        compiler_params=pltpu.CompilerParams(vmem_limit_bytes=40 * 2**20),
+        compiler_params=pltpu.CompilerParams(vmem_limit_bytes=56 * 2**20),
         cost_estimate=pl.CostEstimate(
             flops=60 * hidden * width,
             bytes_accessed=90 * hidden * width,
@@ -857,7 +885,7 @@
         drows.reshape(rows_dec, width),
         rollout,
         dec_line,
-        dec_scale.reshape(1, steps * dec_here),
+        jnp.transpose(dec_scale, (0, 2, 1)),
     )
     return (
         master_new[None],

time: 247 us -> 243 us (0.984)
  local copies, waits for them, and re-layouts: 8.96 us -> 1.64 us
  Pallas kernels: 235 us -> 239 us
    unnamed x9 -> x1, local copies, waits for them, and re-layouts: 7.69 us -> 1.64 us
    pallas_call x1, Pallas kernels: 29.1 us -> 32.2 us  [moved_rows(): pl.pallas_call(adam_kernel, grid=(tall, 3), out_shape=(wide, wide, wide,...]
where the time goes in v4:
time: 243 us; the launch traced here: 242 us
  Pallas kernels  239 us (98%)
    pallas_call x1, Pallas kernels, moved_rows(): pl.pallas_call(functools.partial(learner_kernel, groups, dec_here), out_s...  168 us
    pallas_call x1, Pallas kernels, moved_rows(): pl.pallas_call(functools.partial(decode_kernel, groups, dec_here), out_sh...  38.7 us
    pallas_call x1, Pallas kernels, moved_rows(): pl.pallas_call(adam_kernel, grid=(tall, 3), out_shape=(wide, wide, wide,...  32.2 us

profile of v4, /device:TPU:0, one launch (start us, length us, event | category | flops | bytes accessed | tf_op | source)
XLA Modules:
  0.0 241.6 jit_solution(17176273214064737443)
XLA Ops:
  0.6 168.4 %learner.1 = (bf16[768,3584]{1,0:T(8,128)(2,1)}, bf16[2,8,16,3584]{3,2,1,0:T(8,128)(2,1)}) custom-call(bf16[128,3584]{1,0:T(8,128)(2,1)} %tok.1, bf16[128,3584]{1,0:T(8,128)(2,1)} %cot.1, f32[1,128]{1,0:T(1,128)} %bitcast.30, s32[1,128]{1,0:T(1,128)} %bitcast.31, bf16[64,3584]{1,0:T(8,128)(2,1)} %bitcast.29, s32[4,1,16]{2,1,0:T(1,128)} %bitcast.23, ...), custom_call_target="tpu_custom_call" | custom-call | flops 16911433728 | bytes 22020096 | tf_op jit(solution)/shard_map/learner/pallas_call | solution.py:765
  169.1 32.2 %adam.1 = (f32[256,10752]{1,0:T(8,128)}, f32[256,10752]{1,0:T(8,128)}, f32[256,10752]{1,0:T(8,128)}, bf16[256,10752]{1,0:T(8,128)(2,1)}) custom-call(bf16[768,3584]{1,0:T(8,128)(2,1)} %get-tuple-element.10.grads, f32[256,10752]{1,0:T(8,128)} %bitcast.18, f32[256,10752]{1,0:T(8,128)} %bitcast.19, f32[256,10752]{1,0:T(8,128)} %bitcast.20), custom_call_target="tpu_custom_call" | custom-call | flops 55050240 | bytes 82575360 | tf_op jit(solution)/shard_map/adam/pallas_call | solution.py:833
  201.3 38.7 %decode.1 = bf16[64,1792]{1,0:T(8,128)(2,1)} custom-call(bf16[256,3584]{1,0:T(8,128)(2,1)} %bitcast.21, bf16[256,10752]{1,0:T(8,128)(2,1)} %get-tuple-element.15.roll_in, s32[4,1,16]{2,1,0:T(1,128)} %bitcast.24, f32[4,1,16]{2,1,0:T(1,128)} %bitcast.25), custom_call_target="tpu_custom_call" | custom-call | flops 1409286144 | bytes 5505024 | tf_op jit(solution)/shard_map/decode/pallas_call | solution.py:855
  240.0 1.6 copy.18

commit v5 on v4

--- a/solution.py
+++ b/solution.py
@@ -551,13 +551,12 @@
             for step in range(1, EXPERTS):
                 dnear[step].start()
         pass_on(index)
-        if index == PIECES - 2:
-            for step in range(EXPERTS):
-                beside[step].wait_recv()
-            own = rows.at[1, 0]
-            score_all(own)
-            accumulate(own)
     own = rows.at[0, 1]
+    score_all(own)
+    accumulate(own)
+    for step in range(EXPERTS):
+        beside[step].wait_recv()
+    own = rows.at[1, 0]
     score_all(own)
     accumulate(own)
     own = rows.at[1, 1]

time: 243 us -> 243 us (level)
    pallas_call x1, Pallas kernels: 168 us -> 161 us  [moved_rows(): pl.pallas_call(functools.partial(learner_kernel, groups, dec_here), out_s...]
    pallas_call x1, Pallas kernels: 38.7 us -> 46.6 us  [moved_rows(): pl.pallas_call(functools.partial(decode_kernel, groups, dec_here), out_sh...]
where the time goes in v5:
time: 243 us; the launch traced here: 242 us
  Pallas kernels  239 us (98%)
    pallas_call x1, Pallas kernels, moved_rows(): pl.pallas_call(functools.partial(learner_kernel, groups, dec_here), out_s...  161 us
    pallas_call x1, Pallas kernels, moved_rows(): pl.pallas_call(functools.partial(decode_kernel, groups, dec_here), out_sh...  46.6 us
    pallas_call x1, Pallas kernels, moved_rows(): pl.pallas_call(adam_kernel, grid=(tall, 3), out_shape=(wide, wide, wide,...  32.2 us

profile of v5, /device:TPU:0, one launch (start us, length us, event | category | flops | bytes accessed | tf_op | source)
XLA Modules:
  0.0 241.6 jit_solution(4856238779321944511)
XLA Ops:
  0.6 160.6 %learner.1 = (bf16[768,3584]{1,0:T(8,128)(2,1)}, bf16[2,8,16,3584]{3,2,1,0:T(8,128)(2,1)}) custom-call(bf16[128,3584]{1,0:T(8,128)(2,1)} %tok.1, bf16[128,3584]{1,0:T(8,128)(2,1)} %cot.1, f32[1,128]{1,0:T(1,128)} %bitcast.30, s32[1,128]{1,0:T(1,128)} %bitcast.31, bf16[64,3584]{1,0:T(8,128)(2,1)} %bitcast.29, s32[4,1,16]{2,1,0:T(1,128)} %bitcast.23, ...), custom_call_target="tpu_custom_call" | custom-call | flops 16911433728 | bytes 22020096 | tf_op jit(solution)/shard_map/learner/pallas_call | solution.py:764
  161.2 32.2 %adam.1 = (f32[256,10752]{1,0:T(8,128)}, f32[256,10752]{1,0:T(8,128)}, f32[256,10752]{1,0:T(8,128)}, bf16[256,10752]{1,0:T(8,128)(2,1)}) custom-call(bf16[768,3584]{1,0:T(8,128)(2,1)} %get-tuple-element.10.grads, f32[256,10752]{1,0:T(8,128)} %bitcast.18, f32[256,10752]{1,0:T(8,128)} %bitcast.19, f32[256,10752]{1,0:T(8,128)} %bitcast.20), custom_call_target="tpu_custom_call" | custom-call | flops 55050240 | bytes 82575360 | tf_op jit(solution)/shard_map/adam/pallas_call | solution.py:832
  193.4 46.6 %decode.1 = bf16[64,1792]{1,0:T(8,128)(2,1)} custom-call(bf16[256,3584]{1,0:T(8,128)(2,1)} %bitcast.21, bf16[256,10752]{1,0:T(8,128)(2,1)} %get-tuple-element.15.roll_in, s32[4,1,16]{2,1,0:T(1,128)} %bitcast.24, f32[4,1,16]{2,1,0:T(1,128)} %bitcast.25), custom_call_target="tpu_custom_call" | custom-call | flops 1409286144 | bytes 5505024 | tf_op jit(solution)/shard_map/decode/pallas_call | solution.py:854
  240.0 1.6 copy.18
